TPU v7x, 768 devices: a whole 4x8x12 slice. The times are simulated.
768 devices in a mesh: row: 8 (over z_hi, core), col: 96 (over x, y, z_lo).
Axes of the slice: x: 4, y: 8, z: 12 (z_hi: 4, z_lo: 3; z = z_hi * 3 + z_lo), core: 2. Of those that a mesh axis runs over, the one named last changes fastest.
Arguments:
- left_blocks: bfloat16 [64, 192, 128, 128], P('row', 'col'), may hold values from -6 to 6
- left_columns: int32 [64, 192], P('row', 'col'), may hold values from 0 to 3, as said below
- left_count: int32 [64, 96], P('row', 'col'), may hold values from 1 to 2, as said below
- right_blocks: bfloat16 [32, 192, 128, 128], P('row', 'col'), may hold values from -0.375 to 0.375
- right_columns: int32 [32, 192], P('row', 'col'), may hold values from 0 to 7, as said below
- right_count: int32 [32, 96], P('row', 'col'), may hold values from 1 to 2, as said below
- out_columns: int32 [64, 384], P('row', 'col'), may hold values from 0 to 7, as said below
- out_count: int32 [64, 96], P('row', 'col'), may hold values from 1 to 4, as said below
- atom_owner: int32 [12, 32], replicated, may hold values from 0 to 7, as said below
Outputs:
- product: bfloat16 [64, 384, 128, 128], P('row', 'col')
Inputs may be any that keep to these rules, and one draw needn't show every extreme that they name: `left_columns`: within one row and one grid column the 2 entries are distinct. `left_count`: rows 0, 8, 16 and so on have the full count in every grid column. `right_columns`: within one row and one grid column the 2 entries are distinct. `right_count`: rows 0, 4, 8 and so on have the full count in every grid column. `out_columns`: within one row and one grid column the 4 entries are distinct. `out_count`: rows 0, 8, 16 and so on have the full count in every grid column. `atom_owner`: in each region every owner holds exactly 4 block rows, and the 4 rows of one panel (rows p * 4 to p * 4 + 3) have distinct owners.
All inputs are finite; a program needn't handle non-finite values.
Results may differ from a plain program's by a relative error of at most 0.001.
Values may be sent and summed in bfloat16 or wider, within the bound.
A program may use at most 64 MiB of HBM per device.

v0:
```python
import jax
import jax.numpy as jnp
from jax import lax
from jax.sharding import PartitionSpec as P


def shifted(value, axis, steps):
    count = lax.axis_size(axis)
    pairs = [(source, (source + steps) % count) for source in range(count)]
    return lax.ppermute(value, axis, pairs)


def panel_product(left_state, right_state, out_columns):
    left_blocks, left_columns, left_count = left_state
    right_blocks, right_columns, right_count = right_state
    rows, slots = left_columns.shape
    panel, width = right_columns.shape
    block = right_blocks.shape[-1]
    left_live = lax.broadcasted_iota(jnp.int32, (rows, slots), 1) < left_count
    right_live = lax.broadcasted_iota(jnp.int32, (panel, width), 1) < right_count
    row_columns = right_columns[left_columns]
    row_live = right_live[left_columns]
    match = (row_columns[:, :, None, :] == out_columns[:, None, :, None]) & row_live[:, :, None, :]
    position = jnp.sum(jnp.where(match, lax.broadcasted_iota(jnp.int32, match.shape, 3), 0), axis=3)
    found = jnp.any(match, axis=3) & left_live[:, :, None]
    flat = left_columns[:, :, None] * width + position
    picked = right_blocks.reshape(panel * width, block, block)[flat]
    picked = jnp.where(found[:, :, :, None, None], picked, jnp.zeros((), right_blocks.dtype))
    return jnp.einsum("iaxy,iacyz->icxz", left_blocks, picked, preferred_element_type=jnp.float32)


def body(
    left_blocks,
    left_columns,
    left_count,
    right_blocks,
    right_columns,
    right_count,
    out_columns,
    out_count,
    atom_owner,
):
    grid = lax.axis_size("row")
    regions = lax.axis_size("col") // grid
    grid_row = lax.axis_index("row")
    grid_col = lax.axis_index("col")
    cannon_col = grid_col // regions
    region = grid_col % regions
    panel = right_columns.shape[0]
    owner = lax.dynamic_index_in_dim(atom_owner, region, 0, keepdims=False)
    contract = owner.shape[0]
    order = jnp.arange(contract, dtype=jnp.int32)
    earlier = (owner[:, None] == owner[None, :]) & (order[None, :] < order[:, None])
    rank = jnp.sum(earlier.astype(jnp.int32), axis=1)
    panel_owner = owner.reshape(grid, panel)
    panel_rank = rank.reshape(grid, panel)
    targets = (jnp.arange(grid, dtype=jnp.int32) + cannon_col) % grid
    mine = panel_owner[targets] == grid_row
    local = jnp.sum(jnp.where(mine, panel_rank[targets], 0), axis=1)
    present = jnp.any(mine, axis=1)
    send_blocks = jnp.where(
        present[:, None, None, None], right_blocks[local], jnp.zeros((), right_blocks.dtype)
    )
    send_columns = right_columns[local]
    send_count = jnp.where(present[:, None], right_count[local], 0)
    got_blocks, got_columns, got_count = (
        lax.all_to_all(send_blocks, "row", split_axis=0, concat_axis=0, tiled=True),
        lax.all_to_all(send_columns, "row", split_axis=0, concat_axis=0, tiled=True),
        lax.all_to_all(send_count, "row", split_axis=0, concat_axis=0, tiled=True),
    )
    senders = lax.dynamic_index_in_dim(
        panel_owner, (grid_row + cannon_col) % grid, 0, keepdims=False
    )
    right_now = (got_blocks[senders], got_columns[senders], got_count[senders])
    left_now = (left_blocks, left_columns, left_count)
    total = panel_product(left_now, right_now, out_columns)
    for offset in range(1, grid):
        left_now = shifted((left_now[0], left_now[1], left_now[2]), "col", -regions)
        right_now = shifted((right_now[0], right_now[1], right_now[2]), "row", -1)
        total = total + panel_product(left_now, right_now, out_columns)
    live = lax.broadcasted_iota(jnp.int32, out_columns.shape, 1) < out_count
    return jnp.where(live[:, :, None, None], total, jnp.zeros((), jnp.float32)).astype(jnp.bfloat16)


def solution(mesh):
    placed = (
        P("row", "col", None, None),
        P("row", "col"),
        P("row", "col"),
        P("row", "col", None, None),
        P("row", "col"),
        P("row", "col"),
        P("row", "col"),
        P("row", "col"),
        P(),
    )
    return jax.shard_map(
        body, mesh=mesh, in_specs=placed, out_specs=P("row", "col", None, None), check_vma=False
    )
```

profile of v0, /device:TPU:65, one launch (start us, length us, event | category | flops | bytes accessed | tf_op | source)
XLA Modules:
  0.0 410.1 jit_solution(4818171782541121970)
XLA Ops:
  4.5 14.3 %all-to-all-start.1 = ((s32[8,1,1]{2,1,0:T(1,128)}), s32[8,1,1]{2,1,0:T(1,128)S(1)}, u32[]{:S(2)}, u32[]{:S(2)}) async-start(s32[8,1,1]{2,1,0:T(1,128)} %copy.260), calls=%async_computation.1 | async-start | bytes 8192 | tf_op jit(solution)/shard_map/all_to_all | solution.py:69
  18.8 9.6 %collective-permute-start.1 = (s32[8,2]{0,1:T(2,128)}, s32[8,2]{0,1:T(2,128)S(1)}, u32[]{:S(2)}, u32[]{:S(2)}) collective-permute-start(s32[8,2]{0,1:T(2,128)} %param.10), channel_id=1, source_target_pairs={{0,84},{1,85},{2,86},{3,87},{4,88},{5,89},{6,90},{7,91},{8,92},{9,... | collective-permute-start | bytes 200 | tf_op jit(solution)/shard_map/ppermute | solution.py:10
  30.4 7.5 %collective-permute-start.5 = (bf16[8,2,128,128]{3,2,1,0:T(8,128)(2,1)}, bf16[8,2,128,128]{3,2,1,0:T(8,128)(2,1)S(1)}, u32[]{:S(2)}, u32[]{:S(2)}) collective-permute-start(bf16[8,2,128,128]{3,2,1,0:T(8,128)(2,1)} %param.9), channel_id=1, source_target_pairs={{0,84},{1,85},{2,86},{3,87},{4,88},{5,89},{6,90},{7,91},{8,92},{9,... | collective-permute-start | bytes 1572872 | tf_op jit(solution)/shard_map/ppermute | solution.py:10
  44.6 8.5 %collective-permute-done.9 = s32[8,1]{0,1:T(1,128)S(1)} collective-permute-done((s32[8,1]{0,1:T(1,128)S(1)}, s32[8,1]{0,1:T(1,128)S(1)}, u32[]{:S(2)}, u32[]{:S(2)}) %collective-permute-start.9) | collective-permute-done | bytes 64 | tf_op jit(solution)/shard_map/ppermute | solution.py:10
  53.1 9.6 %collective-permute-start.7 = (s32[8,2]{0,1:T(2,128)S(1)}, s32[8,2]{0,1:T(2,128)S(1)}, u32[]{:S(2)}, u32[]{:S(2)}) collective-permute-start(s32[8,2]{0,1:T(2,128)S(1)} %collective-permute-done.1), channel_id=1, source_target_pairs={{0,84},{1,85},{2,86},{3,87},{4,88},{5,89},{6,90},{7,91},{8,92},{9,... | collective-permute-start | bytes 200 | tf_op jit(solution)/shard_map/ppermute | solution.py:10
  64.6 18.6 %all-to-all-start = ((s32[8,1,2]{2,1,0:T(1,128)}), s32[8,1,2]{2,1,0:T(1,128)S(1)}, u32[]{:S(2)}, u32[]{:S(2)}) async-start(s32[8,1,2]{2,1,0:T(1,128)} %bitcast.92), calls=%async_computation | async-start | bytes 8192 | tf_op jit(solution)/shard_map/all_to_all | solution.py:68
  87.0 6.3 %collective-permute-start.21 = (s32[8,1]{0,1:T(1,128)S(1)}, s32[8,1]{0,1:T(1,128)S(1)}, u32[]{:S(2)}, u32[]{:S(2)}) collective-permute-start(s32[8,1]{0,1:T(1,128)S(1)} %collective-permute-done.15), channel_id=1, source_target_pairs={{0,84},{1,85},{2,86},{3,87},{4,88},{5,89},{6,90},{7,91},{8,92},{9,... | collective-permute-start | bytes 104 | tf_op jit(solution)/shard_map/ppermute | solution.py:10
  94.3 7.0 %collective-permute-start.8 = (s32[4,1]{0,1:T(1,128)S(1)}, s32[4,1]{0,1:T(1,128)S(1)}, u32[]{:S(2)}, u32[]{:S(2)}) collective-permute-start(s32[4,1]{0,1:T(1,128)S(1)} %collective-permute-done.2), channel_id=1, source_target_pairs={{0,672},{96,0},{192,96},{288,192},{384,288},{480,384},{576,480},{6... | collective-permute-start | bytes 56 | tf_op jit(solution)/shard_map/ppermute | solution.py:10
  105.7 4.7 %collective-permute-start.13 = (s32[8,2]{0,1:T(2,128)S(1)}, s32[8,2]{0,1:T(2,128)S(1)}, u32[]{:S(2)}, u32[]{:S(2)}) collective-permute-start(s32[8,2]{0,1:T(2,128)S(1)} %collective-permute-done.7), channel_id=1, source_target_pairs={{0,84},{1,85},{2,86},{3,87},{4,88},{5,89},{6,90},{7,91},{8,92},{9,... | collective-permute-start | bytes 200 | tf_op jit(solution)/shard_map/ppermute | solution.py:10
  115.0 7.1 %collective-permute-start.20 = (s32[4,1]{0,1:T(1,128)S(1)}, s32[4,1]{0,1:T(1,128)S(1)}, u32[]{:S(2)}, u32[]{:S(2)}) collective-permute-start(s32[4,1]{0,1:T(1,128)S(1)} %collective-permute-done.14), channel_id=1, source_target_pairs={{0,672},{96,0},{192,96},{288,192},{384,288},{480,384},{576,480},{6... | collective-permute-start | bytes 56 | tf_op jit(solution)/shard_map/ppermute | solution.py:10
  131.2 5.8 %collective-permute-start.32 = (s32[4,1]{0,1:T(1,128)S(1)}, s32[4,1]{0,1:T(1,128)S(1)}, u32[]{:S(2)}, u32[]{:S(2)}) collective-permute-start(s32[4,1]{0,1:T(1,128)S(1)} %collective-permute-done.26), channel_id=1, source_target_pairs={{0,672},{96,0},{192,96},{288,192},{384,288},{480,384},{576,480},{6... | collective-permute-start | bytes 56 | tf_op jit(solution)/shard_map/ppermute | solution.py:10
  137.0 6.7 %all-to-all-start.2 = ((bf16[8,2,128,128]{3,2,1,0:T(8,128)(2,1)}), bf16[8,2,128,128]{3,2,1,0:T(8,128)(2,1)S(1)}, u32[]{:S(2)}, u32[]{:S(2)}) async-start(bf16[8,2,128,128]{3,2,1,0:T(8,128)(2,1)} %broadcast_select_fusion), calls=%async_computation.2 | async-start | bytes 1048576 | tf_op jit(solution)/shard_map/all_to_all | solution.py:67
  147.0 6.7 %collective-permute-start.38 = (s32[4,1]{0,1:T(1,128)S(1)}, s32[4,1]{0,1:T(1,128)S(1)}, u32[]{:S(2)}, u32[]{:S(2)}) collective-permute-start(s32[4,1]{0,1:T(1,128)S(1)} %collective-permute-done.32), channel_id=1, source_target_pairs={{0,672},{96,0},{192,96},{288,192},{384,288},{480,384},{576,480},{6... | collective-permute-start | bytes 56 | tf_op jit(solution)/shard_map/ppermute | solution.py:10
  154.7 5.8 %collective-permute-start.19 = (s32[8,2]{0,1:T(2,128)S(1)}, s32[8,2]{0,1:T(2,128)S(1)}, u32[]{:S(2)}, u32[]{:S(2)}) collective-permute-start(s32[8,2]{0,1:T(2,128)S(1)} %collective-permute-done.13), channel_id=1, source_target_pairs={{0,84},{1,85},{2,86},{3,87},{4,88},{5,89},{6,90},{7,91},{8,92},{9,... | collective-permute-start | bytes 200 | tf_op jit(solution)/shard_map/ppermute | solution.py:10
  160.6 5.5 %collective-permute-start.39 = (s32[8,1]{0,1:T(1,128)S(1)}, s32[8,1]{0,1:T(1,128)S(1)}, u32[]{:S(2)}, u32[]{:S(2)}) collective-permute-start(s32[8,1]{0,1:T(1,128)S(1)} %collective-permute-done.33), channel_id=1, source_target_pairs={{0,84},{1,85},{2,86},{3,87},{4,88},{5,89},{6,90},{7,91},{8,92},{9,... | collective-permute-start | bytes 104 | tf_op jit(solution)/shard_map/ppermute | solution.py:10
  169.7 5.1 %collective-permute-done.6 = s32[4,2]{1,0:T(4,128)S(1)} collective-permute-done((s32[4,2]{1,0:T(4,128)S(1)}, s32[4,2]{1,0:T(4,128)S(1)}, u32[]{:S(2)}, u32[]{:S(2)}) %collective-permute-start.6) | collective-permute-done | bytes 64 | tf_op jit(solution)/shard_map/ppermute | solution.py:10
  178.4 5.2 %collective-permute-start.25 = (s32[8,2]{0,1:T(2,128)S(1)}, s32[8,2]{0,1:T(2,128)S(1)}, u32[]{:S(2)}, u32[]{:S(2)}) collective-permute-start(s32[8,2]{0,1:T(2,128)S(1)} %collective-permute-done.19), channel_id=1, source_target_pairs={{0,84},{1,85},{2,86},{3,87},{4,88},{5,89},{6,90},{7,91},{8,92},{9,... | collective-permute-start | bytes 200 | tf_op jit(solution)/shard_map/ppermute | solution.py:10
  184.2 6.8 %collective-permute-start.18 = (s32[4,2]{1,0:T(4,128)S(1)}, s32[4,2]{1,0:T(4,128)S(1)}, u32[]{:S(2)}, u32[]{:S(2)}) collective-permute-start(s32[4,2]{1,0:T(4,128)S(1)} %collective-permute-done.12), channel_id=1, source_target_pairs={{0,672},{96,0},{192,96},{288,192},{384,288},{480,384},{576,480},{6... | collective-permute-start | bytes 104 | tf_op jit(solution)/shard_map/ppermute | solution.py:10
  196.1 5.8 %collective-permute-start.31 = (s32[8,2]{0,1:T(2,128)S(1)}, s32[8,2]{0,1:T(2,128)S(1)}, u32[]{:S(2)}, u32[]{:S(2)}) collective-permute-start(s32[8,2]{0,1:T(2,128)S(1)} %collective-permute-done.25), channel_id=1, source_target_pairs={{0,84},{1,85},{2,86},{3,87},{4,88},{5,89},{6,90},{7,91},{8,92},{9,... | collective-permute-start | bytes 200 | tf_op jit(solution)/shard_map/ppermute | solution.py:10
  202.6 6.5 %collective-permute-start.30 = (s32[4,2]{1,0:T(4,128)S(1)}, s32[4,2]{1,0:T(4,128)S(1)}, u32[]{:S(2)}, u32[]{:S(2)}) collective-permute-start(s32[4,2]{1,0:T(4,128)S(1)} %collective-permute-done.24), channel_id=1, source_target_pairs={{0,672},{96,0},{192,96},{288,192},{384,288},{480,384},{576,480},{6... | collective-permute-start | bytes 104 | tf_op jit(solution)/shard_map/ppermute | solution.py:10
  226.0 6.7 %collective-permute-start.11 = (bf16[8,2,128,128]{3,2,1,0:T(8,128)(2,1)S(1)}, bf16[8,2,128,128]{3,2,1,0:T(8,128)(2,1)S(1)}, u32[]{:S(2)}, u32[]{:S(2)}) collective-permute-start(bf16[8,2,128,128]{3,2,1,0:T(8,128)(2,1)S(1)} %collective-permute-done.5), channel_id=1, source_target_pairs={{0,84},{1,85},{2,86},{3,87},{4,88},{5,89},{6,90},{7,91},{8,92},{9,... | collective-permute-start | bytes 1572872 | tf_op jit(solution)/shard_map/ppermute | solution.py:10
  233.1 17.5 %collective-permute-done.11 = bf16[8,2,128,128]{3,2,1,0:T(8,128)(2,1)S(1)} collective-permute-done((bf16[8,2,128,128]{3,2,1,0:T(8,128)(2,1)S(1)}, bf16[8,2,128,128]{3,2,1,0:T(8,128)(2,1)S(1)}, u32[]{:S(2)}, u32[]{:S(2)}) %collective-permute-start.11) | collective-permute-done | bytes 524320 | tf_op jit(solution)/shard_map/ppermute | solution.py:10
  250.6 9.7 %collective-permute-start.17 = (bf16[8,2,128,128]{3,2,1,0:T(8,128)(2,1)S(1)}, bf16[8,2,128,128]{3,2,1,0:T(8,128)(2,1)}, u32[]{:S(2)}, u32[]{:S(2)}) collective-permute-start(bf16[8,2,128,128]{3,2,1,0:T(8,128)(2,1)S(1)} %collective-permute-done.11), channel_id=1, source_target_pairs={{0,84},{1,85},{2,86},{3,87},{4,88},{5,89},{6,90},{7,91},{8,92},{9,... | collective-permute-start | bytes 1572872 | tf_op jit(solution)/shard_map/ppermute | solution.py:10
  260.4 24.2 %collective-permute-done.17 = bf16[8,2,128,128]{3,2,1,0:T(8,128)(2,1)} collective-permute-done((bf16[8,2,128,128]{3,2,1,0:T(8,128)(2,1)S(1)}, bf16[8,2,128,128]{3,2,1,0:T(8,128)(2,1)}, u32[]{:S(2)}, u32[]{:S(2)}) %collective-permute-start.17) | collective-permute-done | bytes 524320 | tf_op jit(solution)/shard_map/ppermute | solution.py:10
  284.6 10.4 %collective-permute-start.23 = (bf16[8,2,128,128]{3,2,1,0:T(8,128)(2,1)}, bf16[8,2,128,128]{3,2,1,0:T(8,128)(2,1)}, u32[]{:S(2)}, u32[]{:S(2)}) collective-permute-start(bf16[8,2,128,128]{3,2,1,0:T(8,128)(2,1)} %collective-permute-done.17), channel_id=1, source_target_pairs={{0,84},{1,85},{2,86},{3,87},{4,88},{5,89},{6,90},{7,91},{8,92},{9,... | collective-permute-start | bytes 1572872 | tf_op jit(solution)/shard_map/ppermute | solution.py:10
  302.0 8.1 %collective-permute-done.4 = bf16[4,2,128,128]{3,2,1,0:T(8,128)(2,1)S(1)} collective-permute-done((bf16[4,2,128,128]{3,2,1,0:T(8,128)(2,1)S(1)}, bf16[4,2,128,128]{3,2,1,0:T(8,128)(2,1)S(1)}, u32[]{:S(2)}, u32[]{:S(2)}) %collective-permute-start.4) | collective-permute-done | bytes 262176 | tf_op jit(solution)/shard_map/ppermute | solution.py:10
  313.0 7.0 %collective-permute-start.29 = (bf16[8,2,128,128]{3,2,1,0:T(8,128)(2,1)}, bf16[8,2,128,128]{3,2,1,0:T(8,128)(2,1)}, u32[]{:S(2)}, u32[]{:S(2)}) collective-permute-start(bf16[8,2,128,128]{3,2,1,0:T(8,128)(2,1)} %collective-permute-done.23), channel_id=1, source_target_pairs={{0,84},{1,85},{2,86},{3,87},{4,88},{5,89},{6,90},{7,91},{8,92},{9,... | collective-permute-start | bytes 1572872 | tf_op jit(solution)/shard_map/ppermute | solution.py:10
  329.5 10.0 %collective-permute-done.16 = bf16[4,2,128,128]{3,2,1,0:T(8,128)(2,1)S(1)} collective-permute-done((bf16[4,2,128,128]{3,2,1,0:T(8,128)(2,1)S(1)}, bf16[4,2,128,128]{3,2,1,0:T(8,128)(2,1)S(1)}, u32[]{:S(2)}, u32[]{:S(2)}) %collective-permute-start.16) | collective-permute-done | bytes 262176 | tf_op jit(solution)/shard_map/ppermute | solution.py:10
  358.9 11.0 %collective-permute-done.28 = bf16[4,2,128,128]{3,2,1,0:T(8,128)(2,1)S(1)} collective-permute-done((bf16[4,2,128,128]{3,2,1,0:T(8,128)(2,1)S(1)}, bf16[4,2,128,128]{3,2,1,0:T(8,128)(2,1)S(1)}, u32[]{:S(2)}, u32[]{:S(2)}) %collective-permute-start.28) | collective-permute-done | bytes 262176 | tf_op jit(solution)/shard_map/ppermute | solution.py:10
  378.0 6.5 %collective-permute-done.34 = bf16[4,2,128,128]{3,2,1,0:T(8,128)(2,1)S(1)} collective-permute-done((bf16[4,2,128,128]{3,2,1,0:T(8,128)(2,1)S(1)}, bf16[4,2,128,128]{3,2,1,0:T(8,128)(2,1)S(1)}, u32[]{:S(2)}, u32[]{:S(2)}) %collective-permute-start.34) | collective-permute-done | bytes 262176 | tf_op jit(solution)/shard_map/ppermute | solution.py:10
  389.6 9.5 %collective-permute-done.40 = bf16[4,2,128,128]{3,2,1,0:T(8,128)(2,1)S(1)} collective-permute-done((bf16[4,2,128,128]{3,2,1,0:T(8,128)(2,1)S(1)}, bf16[4,2,128,128]{3,2,1,0:T(8,128)(2,1)S(1)}, u32[]{:S(2)}, u32[]{:S(2)}) %collective-permute-start.40) | collective-permute-done | bytes 262176 | tf_op jit(solution)/shard_map/ppermute | solution.py:10
  400.1 7.7 %fusion.28 = bf16[8,4,128,128]{2,3,1,0:T(8,128)(2,1)} fusion(bf16[8,2,4,128,128]{4,3,2,1,0:T(8,128)(2,1)S(1)} %bitcast.270, pred[8,2,4]{2,1,0:T(4,128)(4,1)S(1)} %copy.319, f32[8,4,128,128,1]{3,2,1,4,0:T(8,128)} %fusion.4, f32[8,4,128,128,1]{3,2,1,4,0:T(8,128)} %fusion.6, f32[8,4,128,128,1]{3,2,1,4,0:T(8,128)} %fusion.8, ...), kind=kOutput, calls=%fused_computation.65 | convolution fusion | flops 274202624 | bytes 18350176 | tf_op jit(solution)/shard_map/iaxy,iacyz->icxz/dot_general | solution.py:29
  (261 shorter events, 127.7 us)
Async XLA Ops:
  4.5 60.1 %all-to-all-start.1 = ((s32[8,1,1]{2,1,0:T(1,128)}), s32[8,1,1]{2,1,0:T(1,128)S(1)}, u32[]{:S(2)}, u32[]{:S(2)}) async-start(s32[8,1,1]{2,1,0:T(1,128)} %copy.260), calls=%async_computation.1 | async-start | bytes 8192 | tf_op jit(solution)/shard_map/all_to_all | solution.py:69
  18.8 25.5 %collective-permute-start.1 = (s32[8,2]{0,1:T(2,128)}, s32[8,2]{0,1:T(2,128)S(1)}, u32[]{:S(2)}, u32[]{:S(2)}) collective-permute-start(s32[8,2]{0,1:T(2,128)} %param.10), channel_id=1, source_target_pairs={{0,84},{1,85},{2,86},{3,87},{4,88},{5,89},{6,90},{7,91},{8,92},{9,... | collective-permute-start | bytes 200 | tf_op jit(solution)/shard_map/ppermute | solution.py:10
  28.5 13.9 %collective-permute-start.3 = (s32[8,1]{0,1:T(1,128)}, s32[8,1]{0,1:T(1,128)S(1)}, u32[]{:S(2)}, u32[]{:S(2)}) collective-permute-start(s32[8,1]{0,1:T(1,128)} %param.11), channel_id=1, source_target_pairs={{0,84},{1,85},{2,86},{3,87},{4,88},{5,89},{6,90},{7,91},{8,92},{9,... | collective-permute-start | bytes 104 | tf_op jit(solution)/shard_map/ppermute | solution.py:10
  30.4 195.5 %collective-permute-start.5 = (bf16[8,2,128,128]{3,2,1,0:T(8,128)(2,1)}, bf16[8,2,128,128]{3,2,1,0:T(8,128)(2,1)S(1)}, u32[]{:S(2)}, u32[]{:S(2)}) collective-permute-start(bf16[8,2,128,128]{3,2,1,0:T(8,128)(2,1)} %param.9), channel_id=1, source_target_pairs={{0,84},{1,85},{2,86},{3,87},{4,88},{5,89},{6,90},{7,91},{8,92},{9,... | collective-permute-start | bytes 1572872 | tf_op jit(solution)/shard_map/ppermute | solution.py:10
  53.1 51.5 %collective-permute-start.7 = (s32[8,2]{0,1:T(2,128)S(1)}, s32[8,2]{0,1:T(2,128)S(1)}, u32[]{:S(2)}, u32[]{:S(2)}) collective-permute-start(s32[8,2]{0,1:T(2,128)S(1)} %collective-permute-done.1), channel_id=1, source_target_pairs={{0,84},{1,85},{2,86},{3,87},{4,88},{5,89},{6,90},{7,91},{8,92},{9,... | collective-permute-start | bytes 200 | tf_op jit(solution)/shard_map/ppermute | solution.py:10
  62.7 24.3 %collective-permute-start.15 = (s32[8,1]{0,1:T(1,128)S(1)}, s32[8,1]{0,1:T(1,128)S(1)}, u32[]{:S(2)}, u32[]{:S(2)}) collective-permute-start(s32[8,1]{0,1:T(1,128)S(1)} %collective-permute-done.9), channel_id=1, source_target_pairs={{0,84},{1,85},{2,86},{3,87},{4,88},{5,89},{6,90},{7,91},{8,92},{9,... | collective-permute-start | bytes 104 | tf_op jit(solution)/shard_map/ppermute | solution.py:10
  64.6 72.4 %all-to-all-start = ((s32[8,1,2]{2,1,0:T(1,128)}), s32[8,1,2]{2,1,0:T(1,128)S(1)}, u32[]{:S(2)}, u32[]{:S(2)}) async-start(s32[8,1,2]{2,1,0:T(1,128)} %bitcast.92), calls=%async_computation | async-start | bytes 8192 | tf_op jit(solution)/shard_map/all_to_all | solution.py:68
  87.0 18.7 %collective-permute-start.21 = (s32[8,1]{0,1:T(1,128)S(1)}, s32[8,1]{0,1:T(1,128)S(1)}, u32[]{:S(2)}, u32[]{:S(2)}) collective-permute-start(s32[8,1]{0,1:T(1,128)S(1)} %collective-permute-done.15), channel_id=1, source_target_pairs={{0,84},{1,85},{2,86},{3,87},{4,88},{5,89},{6,90},{7,91},{8,92},{9,... | collective-permute-start | bytes 104 | tf_op jit(solution)/shard_map/ppermute | solution.py:10
  102.5 12.4 %collective-permute-start.14 = (s32[4,1]{0,1:T(1,128)S(1)}, s32[4,1]{0,1:T(1,128)S(1)}, u32[]{:S(2)}, u32[]{:S(2)}) collective-permute-start(s32[4,1]{0,1:T(1,128)S(1)} %collective-permute-done.8), channel_id=1, source_target_pairs={{0,672},{96,0},{192,96},{288,192},{384,288},{480,384},{576,480},{6... | collective-permute-start | bytes 56 | tf_op jit(solution)/shard_map/ppermute | solution.py:10
  105.7 47.9 %collective-permute-start.13 = (s32[8,2]{0,1:T(2,128)S(1)}, s32[8,2]{0,1:T(2,128)S(1)}, u32[]{:S(2)}, u32[]{:S(2)}) collective-permute-start(s32[8,2]{0,1:T(2,128)S(1)} %collective-permute-done.7), channel_id=1, source_target_pairs={{0,84},{1,85},{2,86},{3,87},{4,88},{5,89},{6,90},{7,91},{8,92},{9,... | collective-permute-start | bytes 200 | tf_op jit(solution)/shard_map/ppermute | solution.py:10
  110.4 15.0 %collective-permute-start.27 = (s32[8,1]{0,1:T(1,128)S(1)}, s32[8,1]{0,1:T(1,128)S(1)}, u32[]{:S(2)}, u32[]{:S(2)}) collective-permute-start(s32[8,1]{0,1:T(1,128)S(1)} %collective-permute-done.21), channel_id=1, source_target_pairs={{0,84},{1,85},{2,86},{3,87},{4,88},{5,89},{6,90},{7,91},{8,92},{9,... | collective-permute-start | bytes 104 | tf_op jit(solution)/shard_map/ppermute | solution.py:10
  125.4 35.2 %collective-permute-start.33 = (s32[8,1]{0,1:T(1,128)S(1)}, s32[8,1]{0,1:T(1,128)S(1)}, u32[]{:S(2)}, u32[]{:S(2)}) collective-permute-start(s32[8,1]{0,1:T(1,128)S(1)} %collective-permute-done.27), channel_id=1, source_target_pairs={{0,84},{1,85},{2,86},{3,87},{4,88},{5,89},{6,90},{7,91},{8,92},{9,... | collective-permute-start | bytes 104 | tf_op jit(solution)/shard_map/ppermute | solution.py:10
  131.2 15.7 %collective-permute-start.32 = (s32[4,1]{0,1:T(1,128)S(1)}, s32[4,1]{0,1:T(1,128)S(1)}, u32[]{:S(2)}, u32[]{:S(2)}) collective-permute-start(s32[4,1]{0,1:T(1,128)S(1)} %collective-permute-done.26), channel_id=1, source_target_pairs={{0,672},{96,0},{192,96},{288,192},{384,288},{480,384},{576,480},{6... | collective-permute-start | bytes 56 | tf_op jit(solution)/shard_map/ppermute | solution.py:10
  137.0 158.0 %all-to-all-start.2 = ((bf16[8,2,128,128]{3,2,1,0:T(8,128)(2,1)}), bf16[8,2,128,128]{3,2,1,0:T(8,128)(2,1)S(1)}, u32[]{:S(2)}, u32[]{:S(2)}) async-start(bf16[8,2,128,128]{3,2,1,0:T(8,128)(2,1)} %broadcast_select_fusion), calls=%async_computation.2 | async-start | bytes 1048576 | tf_op jit(solution)/shard_map/all_to_all | solution.py:67
  144.3 21.9 %collective-permute-start = (s32[4,2]{1,0:T(4,128)S(1)}, s32[4,2]{1,0:T(4,128)S(1)}, u32[]{:S(2)}, u32[]{:S(2)}) collective-permute-start(s32[4,2]{1,0:T(4,128)S(1)} %gather_fusion.3), channel_id=1, source_target_pairs={{0,672},{96,0},{192,96},{288,192},{384,288},{480,384},{576,480},{6... | collective-permute-start | bytes 104 | tf_op jit(solution)/shard_map/ppermute | solution.py:10
  147.0 19.1 %collective-permute-start.38 = (s32[4,1]{0,1:T(1,128)S(1)}, s32[4,1]{0,1:T(1,128)S(1)}, u32[]{:S(2)}, u32[]{:S(2)}) collective-permute-start(s32[4,1]{0,1:T(1,128)S(1)} %collective-permute-done.32), channel_id=1, source_target_pairs={{0,672},{96,0},{192,96},{288,192},{384,288},{480,384},{576,480},{6... | collective-permute-start | bytes 56 | tf_op jit(solution)/shard_map/ppermute | solution.py:10
  154.7 22.6 %collective-permute-start.19 = (s32[8,2]{0,1:T(2,128)S(1)}, s32[8,2]{0,1:T(2,128)S(1)}, u32[]{:S(2)}, u32[]{:S(2)}) collective-permute-start(s32[8,2]{0,1:T(2,128)S(1)} %collective-permute-done.13), channel_id=1, source_target_pairs={{0,84},{1,85},{2,86},{3,87},{4,88},{5,89},{6,90},{7,91},{8,92},{9,... | collective-permute-start | bytes 200 | tf_op jit(solution)/shard_map/ppermute | solution.py:10
  178.4 16.6 %collective-permute-start.25 = (s32[8,2]{0,1:T(2,128)S(1)}, s32[8,2]{0,1:T(2,128)S(1)}, u32[]{:S(2)}, u32[]{:S(2)}) collective-permute-start(s32[8,2]{0,1:T(2,128)S(1)} %collective-permute-done.19), channel_id=1, source_target_pairs={{0,84},{1,85},{2,86},{3,87},{4,88},{5,89},{6,90},{7,91},{8,92},{9,... | collective-permute-start | bytes 200 | tf_op jit(solution)/shard_map/ppermute | solution.py:10
  196.1 16.6 %collective-permute-start.31 = (s32[8,2]{0,1:T(2,128)S(1)}, s32[8,2]{0,1:T(2,128)S(1)}, u32[]{:S(2)}, u32[]{:S(2)}) collective-permute-start(s32[8,2]{0,1:T(2,128)S(1)} %collective-permute-done.25), channel_id=1, source_target_pairs={{0,84},{1,85},{2,86},{3,87},{4,88},{5,89},{6,90},{7,91},{8,92},{9,... | collective-permute-start | bytes 200 | tf_op jit(solution)/shard_map/ppermute | solution.py:10
  210.7 12.3 %collective-permute-start.36 = (s32[4,2]{1,0:T(4,128)S(1)}, s32[4,2]{1,0:T(4,128)S(1)}, u32[]{:S(2)}, u32[]{:S(2)}) collective-permute-start(s32[4,2]{1,0:T(4,128)S(1)} %collective-permute-done.30), channel_id=1, source_target_pairs={{0,672},{96,0},{192,96},{288,192},{384,288},{480,384},{576,480},{6... | collective-permute-start | bytes 104 | tf_op jit(solution)/shard_map/ppermute | solution.py:10
  226.0 24.6 %collective-permute-start.11 = (bf16[8,2,128,128]{3,2,1,0:T(8,128)(2,1)S(1)}, bf16[8,2,128,128]{3,2,1,0:T(8,128)(2,1)S(1)}, u32[]{:S(2)}, u32[]{:S(2)}) collective-permute-start(bf16[8,2,128,128]{3,2,1,0:T(8,128)(2,1)S(1)} %collective-permute-done.5), channel_id=1, source_target_pairs={{0,84},{1,85},{2,86},{3,87},{4,88},{5,89},{6,90},{7,91},{8,92},{9,... | collective-permute-start | bytes 1572872 | tf_op jit(solution)/shard_map/ppermute | solution.py:10
  250.6 34.0 %collective-permute-start.17 = (bf16[8,2,128,128]{3,2,1,0:T(8,128)(2,1)S(1)}, bf16[8,2,128,128]{3,2,1,0:T(8,128)(2,1)}, u32[]{:S(2)}, u32[]{:S(2)}) collective-permute-start(bf16[8,2,128,128]{3,2,1,0:T(8,128)(2,1)S(1)} %collective-permute-done.11), channel_id=1, source_target_pairs={{0,84},{1,85},{2,86},{3,87},{4,88},{5,89},{6,90},{7,91},{8,92},{9,... | collective-permute-start | bytes 1572872 | tf_op jit(solution)/shard_map/ppermute | solution.py:10
  284.6 28.4 %collective-permute-start.23 = (bf16[8,2,128,128]{3,2,1,0:T(8,128)(2,1)}, bf16[8,2,128,128]{3,2,1,0:T(8,128)(2,1)}, u32[]{:S(2)}, u32[]{:S(2)}) collective-permute-start(bf16[8,2,128,128]{3,2,1,0:T(8,128)(2,1)} %collective-permute-done.17), channel_id=1, source_target_pairs={{0,84},{1,85},{2,86},{3,87},{4,88},{5,89},{6,90},{7,91},{8,92},{9,... | collective-permute-start | bytes 1572872 | tf_op jit(solution)/shard_map/ppermute | solution.py:10
  295.7 14.4 %collective-permute-start.4 = (bf16[4,2,128,128]{3,2,1,0:T(8,128)(2,1)S(1)}, bf16[4,2,128,128]{3,2,1,0:T(8,128)(2,1)S(1)}, u32[]{:S(2)}, u32[]{:S(2)}) collective-permute-start(bf16[4,2,128,128]{3,2,1,0:T(8,128)(2,1)S(1)} %gather_fusion.9), channel_id=1, source_target_pairs={{0,672},{96,0},{192,96},{288,192},{384,288},{480,384},{576,480},{6... | collective-permute-start | bytes 786440 | tf_op jit(solution)/shard_map/ppermute | solution.py:10
  311.1 13.0 %collective-permute-start.10 = (bf16[4,2,128,128]{3,2,1,0:T(8,128)(2,1)S(1)}, bf16[4,2,128,128]{3,2,1,0:T(8,128)(2,1)S(1)}, u32[]{:S(2)}, u32[]{:S(2)}) collective-permute-start(bf16[4,2,128,128]{3,2,1,0:T(8,128)(2,1)S(1)} %collective-permute-done.4), channel_id=1, source_target_pairs={{0,672},{96,0},{192,96},{288,192},{384,288},{480,384},{576,480},{6... | collective-permute-start | bytes 786440 | tf_op jit(solution)/shard_map/ppermute | solution.py:10
  313.0 29.4 %collective-permute-start.29 = (bf16[8,2,128,128]{3,2,1,0:T(8,128)(2,1)}, bf16[8,2,128,128]{3,2,1,0:T(8,128)(2,1)}, u32[]{:S(2)}, u32[]{:S(2)}) collective-permute-start(bf16[8,2,128,128]{3,2,1,0:T(8,128)(2,1)} %collective-permute-done.23), channel_id=1, source_target_pairs={{0,84},{1,85},{2,86},{3,87},{4,88},{5,89},{6,90},{7,91},{8,92},{9,... | collective-permute-start | bytes 1572872 | tf_op jit(solution)/shard_map/ppermute | solution.py:10
  325.0 14.5 %collective-permute-start.16 = (bf16[4,2,128,128]{3,2,1,0:T(8,128)(2,1)S(1)}, bf16[4,2,128,128]{3,2,1,0:T(8,128)(2,1)S(1)}, u32[]{:S(2)}, u32[]{:S(2)}) collective-permute-start(bf16[4,2,128,128]{3,2,1,0:T(8,128)(2,1)S(1)} %collective-permute-done.10), channel_id=1, source_target_pairs={{0,672},{96,0},{192,96},{288,192},{384,288},{480,384},{576,480},{6... | collective-permute-start | bytes 786440 | tf_op jit(solution)/shard_map/ppermute | solution.py:10
  342.4 30.3 %collective-permute-start.35 = (bf16[8,2,128,128]{3,2,1,0:T(8,128)(2,1)}, bf16[8,2,128,128]{3,2,1,0:T(8,128)(2,1)S(1)}, u32[]{:S(2)}, u32[]{:S(2)}) collective-permute-start(bf16[8,2,128,128]{3,2,1,0:T(8,128)(2,1)} %collective-permute-done.29), channel_id=1, source_target_pairs={{0,84},{1,85},{2,86},{3,87},{4,88},{5,89},{6,90},{7,91},{8,92},{9,... | collective-permute-start | bytes 1572872 | tf_op jit(solution)/shard_map/ppermute | solution.py:10
  353.6 16.2 %collective-permute-start.28 = (bf16[4,2,128,128]{3,2,1,0:T(8,128)(2,1)S(1)}, bf16[4,2,128,128]{3,2,1,0:T(8,128)(2,1)S(1)}, u32[]{:S(2)}, u32[]{:S(2)}) collective-permute-start(bf16[4,2,128,128]{3,2,1,0:T(8,128)(2,1)S(1)} %collective-permute-done.22), channel_id=1, source_target_pairs={{0,672},{96,0},{192,96},{288,192},{384,288},{480,384},{576,480},{6... | collective-permute-start | bytes 786440 | tf_op jit(solution)/shard_map/ppermute | solution.py:10
  370.8 13.7 %collective-permute-start.34 = (bf16[4,2,128,128]{3,2,1,0:T(8,128)(2,1)S(1)}, bf16[4,2,128,128]{3,2,1,0:T(8,128)(2,1)S(1)}, u32[]{:S(2)}, u32[]{:S(2)}) collective-permute-start(bf16[4,2,128,128]{3,2,1,0:T(8,128)(2,1)S(1)} %collective-permute-done.28), channel_id=1, source_target_pairs={{0,672},{96,0},{192,96},{288,192},{384,288},{480,384},{576,480},{6... | collective-permute-start | bytes 786440 | tf_op jit(solution)/shard_map/ppermute | solution.py:10
  372.8 27.3 %collective-permute-start.41 = (bf16[8,2,128,128]{3,2,1,0:T(8,128)(2,1)S(1)}, bf16[8,2,128,128]{3,2,1,0:T(8,128)(2,1)}, u32[]{:S(2)}, u32[]{:S(2)}) collective-permute-start(bf16[8,2,128,128]{3,2,1,0:T(8,128)(2,1)S(1)} %collective-permute-done.35), channel_id=1, source_target_pairs={{0,84},{1,85},{2,86},{3,87},{4,88},{5,89},{6,90},{7,91},{8,92},{9,... | collective-permute-start | bytes 1572872 | tf_op jit(solution)/shard_map/ppermute | solution.py:10
  385.4 13.7 %collective-permute-start.40 = (bf16[4,2,128,128]{3,2,1,0:T(8,128)(2,1)S(1)}, bf16[4,2,128,128]{3,2,1,0:T(8,128)(2,1)S(1)}, u32[]{:S(2)}, u32[]{:S(2)}) collective-permute-start(bf16[4,2,128,128]{3,2,1,0:T(8,128)(2,1)S(1)} %collective-permute-done.34), channel_id=1, source_target_pairs={{0,672},{96,0},{192,96},{288,192},{384,288},{480,384},{576,480},{6... | collective-permute-start | bytes 786440 | tf_op jit(solution)/shard_map/ppermute | solution.py:10
  (22 other events, 553.8 us)
where the time goes:
time: 412 us; the launch traced here: 410 us
  starting transfers between devices  229 us (56%)
  waiting for transfers between devices  115 us (28%)
  local copies, waits for them, and re-layouts  34.3 us (8%)
  matrix products  26.6 us (6%)
    ppermute x42, starting transfers between devices, shifted(): return lax.ppermute(value, axis, pairs)  190 us
    ppermute x42, waiting for transfers between devices, shifted(): return lax.ppermute(value, axis, pairs)  115 us
    dot_general x8, matrix products, panel_product(): jnp.einsum('iaxy,iacyz->icxz', left_blocks, picked, preferred_element_typ...  26.6 us
    all_to_all x1, starting transfers between devices, body(): lax.all_to_all(send_columns, 'row', split_axis=0, concat_axis=0, tiled=True)  18.6 us
    all_to_all x1, starting transfers between devices, body(): lax.all_to_all(send_count, 'row', split_axis=0, concat_axis=0, tiled=True)  14.3 us
  transfers between devices with their start and end apart: 45, of which 17 were waited for; matrix products, arithmetic and copies ran while one was open for 12% of the time, Pallas kernels for 0%

commit v1 on v0

v1 whole, which is shorter than its diff:
```python
import functools

import jax
import jax.numpy as jnp
from jax import lax
from jax.experimental import pallas as pl
from jax.experimental.pallas import tpu as pltpu
from jax.sharding import PartitionSpec as P

MESH = pl.DeviceIdType.MESH
ROWS, SLOTS, OUT, PANEL, BLOCK = 8, 2, 4, 4, 128
HALF = ROWS // 2
STEP = 2
N_COPIES = 160
ZERO = 64
PARTS = ("x", "y", "z", "meta", "compute")


def kernel(
    parts,
    left_hbm, lcol, lcount, right_hbm, rcol, rcount, ocol, ocount, owner,
    out_hbm,
    left, relay, right, acc, stage,
    lcode, rcode, ocode, place, pick,
    send_sem, recv_sem, local_sem, out_sem,
):
    r = lax.axis_index("row")
    c = lax.axis_index("col")
    z, core = r // 2, r % 2
    x, y, low = c // 24, (c // 3) % 8, c % 3

    def at_q(dx, dy):
        return (r, ((x + dx) % 4) * 24 + ((y + dy) % 8) * 3 + low)

    def at_row(dz, dcore):
        return (((z + dz) % 4) * 2 + (core + dcore) % 2, c)

    q_peers = [(dy * 4 + dx, at_q(dx, 4 * dy)) for dy in range(2) for dx in range(4)][1:]
    row_peers = [(dz * 2 + dc, at_row(dz, dc)) for dz in range(4) for dc in range(2)][1:]
    east, west = at_q(1, 0), at_q(3, 0)
    north, south = at_q(0, 2), at_q(0, 6)
    up, down, twin = at_row(1, 0), at_row(3, 0), at_row(0, 1)

    barrier = pltpu.get_barrier_semaphore()
    greeted = [d for _, d in q_peers] + [d for _, d in row_peers] + [north, south]
    for device in greeted:
        pl.semaphore_signal(barrier, inc=1, device_id=device, device_id_type=MESH)
    own_left = pltpu.make_async_copy(left_hbm, left.at[0], local_sem.at[0])
    own_left.start()
    own_right = pltpu.make_async_copy(right_hbm, right.at[pl.ds(0, 8)], local_sem.at[1])
    own_right.start()
    for i in range(ROWS):
        for s in range(SLOTS):
            lcode[0, i * 2 + s] = jnp.where(s < lcount[i, 0], lcol[i, s], -1)
        for t in range(OUT):
            ocode[i * 4 + t] = jnp.where(t < ocount[i, 0], ocol[i, t], -1)
    for k in range(PANEL):
        for s in range(2):
            rcode[0, k * 2 + s] = jnp.where(s < rcount[k, 0], rcol[k, s], -2)
    pl.semaphore_wait(barrier, len(greeted))

    sent = []

    def remote(src, dst, device):
        n = len(sent)
        copy = pltpu.make_async_remote_copy(
            src_ref=src, dst_ref=dst, send_sem=send_sem.at[n], recv_sem=recv_sem.at[n],
            device_id=device, device_id_type=MESH,
        )
        copy.start()
        sent.append(copy)
        return copy

    def rows(first):
        return pl.ds(first, STEP)

    alpha = list(range(0, HALF, STEP))
    beta = list(range(HALF, ROWS, STEP))
    n = len(alpha)
    events = []
    waits = {d: [] for d in range(8)}
    right_waits = []

    def ring(d, first, east_copy, west_copy, when):
        if first in alpha:
            def forward():
                east_copy.wait_recv()
                waits[d + 2].append((first, remote(left.at[d + 3, rows(first)], left.at[d + 2, rows(first)], east)))
            events.append((when, forward))
            waits[d + 1].append((first, west_copy))
        else:
            def forward():
                west_copy.wait_recv()
                waits[d + 2].append((first, remote(left.at[d + 1, rows(first)], left.at[d + 2, rows(first)], west)))
            events.append((when, forward))
            waits[d + 3].append((first, east_copy))

    if "y" in parts:
        relayed = []
        for j in range(n):
            relayed.append((
                remote(left_hbm.at[rows(alpha[j])], relay.at[rows(alpha[j])], north),
                remote(left_hbm.at[rows(beta[j])], relay.at[rows(beta[j])], south)))
    if "x" in parts:
        ecopies, wcopies = {}, {}
        for a, b in zip(alpha + beta, beta + alpha):
            ecopies[a] = remote(left_hbm.at[rows(a)], left.at[3, rows(a)], east)
            wcopies[b] = remote(left_hbm.at[rows(b)], left.at[1, rows(b)], west)
        for j in range(n):
            ring(0, alpha[j], ecopies[alpha[j]], wcopies[alpha[j]], 5.2 * (j + 1) / n)
            ring(0, beta[j], ecopies[beta[j]], wcopies[beta[j]], 5.2 * (j + 1) / n)
    if "z" in parts:
        zparts = [(0, 4), (4, 4)]
        ucopies, dcopies = {}, {}
        for a, b in zip(zparts, zparts[::-1]):
            ucopies[a] = remote(right_hbm.at[pl.ds(*a)], right.at[pl.ds(48 + a[0], a[1])], up)
            dcopies[b] = remote(right_hbm.at[pl.ds(*b)], right.at[pl.ds(16 + b[0], b[1])], down)
        right_waits.append(remote(right_hbm, right.at[pl.ds(8, 8)], twin))

        def share(copy, at, size):
            copy.wait_recv()
            right_waits.append(remote(right.at[pl.ds(at, size)], right.at[pl.ds(at + 8, size)], twin))

        def zring(copy, at, size, to, when, on):
            def forward():
                copy.wait_recv()
                if on is not None:
                    passed = remote(right.at[pl.ds(at, size)], right.at[pl.ds(to, size)], on)
                    events2.append((passed, to, size))
                right_waits.append(remote(right.at[pl.ds(at, size)], right.at[pl.ds(at + 8, size)], twin))
            events.append((when, forward))

        events2 = []
        a, b = zparts
        zring(ucopies[a], 48 + a[0], a[1], 32 + a[0], 8.0, up)
        zring(dcopies[b], 16 + b[0], b[1], 32 + b[0], 8.0, down)
        zring(ucopies[b], 48 + b[0], b[1], None, 16.0, None)
        zring(dcopies[a], 16 + a[0], a[1], None, 16.0, None)

        def last():
            for passed, to, size in events2:
                share(passed, to, size)
        events.append((24.0, last))
    if "meta" in parts:
        metas = [remote(lcode.at[0], lcode.at[slot_of(d)], device) for d, device in q_peers]
        metas += [remote(rcode.at[0], rcode.at[slot_of_row(d)], device) for d, device in row_peers]

        def indices():
            region = (y % 4) * 3 + low

            @pl.loop(0, 32)
            def _(k):
                o = owner[region, k]
                rank = jnp.int32(0)
                for e in range(32):
                    rank += jnp.where((owner[region, e] == o) & (e < k), 1, 0)
                oz, oc = o // 2, o % 2
                place[k] = (((oz - z + 4) % 4) * 2 + (oc + core) % 2) * 4 + jnp.minimum(rank, 3)

            for copy in metas:
                copy.wait_recv()

            @pl.loop(0, 64)
            def _(n):
                d, i = n // 8, n % 8
                q = ((x + d % 4) % 4) * 2 + (y // 4 + d // 4) % 2
                panel = (r + q) % 8
                for s in range(SLOTS):
                    j = lcode[d, i * 2 + s]
                    m = place[panel * 4 + jnp.maximum(j, 0)]
                    c0 = jnp.where(j < 0, -3, rcode[m // 4, (m % 4) * 2])
                    c1 = jnp.where(j < 0, -3, rcode[m // 4, (m % 4) * 2 + 1])
                    for t in range(OUT):
                        o = ocode[i * 4 + t]
                        pick[(n * 2 + s) * 4 + t] = jnp.where(o == c0, 2 * m, jnp.where(o == c1, 2 * m + 1, ZERO))
        events.append((6.0, indices))
    if "y" in parts:
        arrived = []

        def pass_on(j):
            def run():
                a, b = relayed[j]
                a.wait_recv()
                p = remote(relay.at[rows(alpha[j])], left.at[4, rows(alpha[j])], north)
                b.wait_recv()
                m = remote(relay.at[rows(beta[j])], left.at[4, rows(beta[j])], south)
                arrived.append((p, m))
            return run

        def spread(j):
            def run():
                p, m = arrived[j]
                fs = []
                for copy, first in ((p, alpha[j]), (m, beta[j])):
                    copy.wait_recv()
                    if "x" in parts:
                        e = remote(left.at[4, rows(first)], left.at[7, rows(first)], east)
                        w = remote(left.at[4, rows(first)], left.at[5, rows(first)], west)
                        fs.append((first, e, w))
                later.append(fs)
            return run

        later = []

        def finish(j):
            def run():
                todo = []
                for first, e, w in later[j]:
                    if first in alpha:
                        e.wait_recv()
                        waits[6].append((first, remote(left.at[7, rows(first)], left.at[6, rows(first)], east)))
                        waits[5].append((first, w))
                    else:
                        w.wait_recv()
                        waits[6].append((first, remote(left.at[5, rows(first)], left.at[6, rows(first)], west)))
                        waits[7].append((first, e))
            return run

        for j in range(n):
            events.append((10.5 * (j + 1) / n, pass_on(j)))
            events.append((10.5 + 10.5 * (j + 1) / n, spread(j)))
            events.append((16 + 10.5 * (j + 1) / n, finish(j)))

    for _, run in sorted(events, key=lambda e: e[0]):
        run()

    own_left.wait()
    own_right.wait()
    right[ZERO] = jnp.zeros((BLOCK, BLOCK), jnp.bfloat16)
    for copy in right_waits:
        copy.wait_recv()
    for d in range(8):
        for _, copy in waits[d]:
            copy.wait_recv()

    if "compute" in parts:
        @pl.loop(0, ROWS)
        def _(i):
            lhs = jnp.concatenate([left[d, i, s] for d in range(8) for s in range(SLOTS)], axis=1)
            rhs = jnp.concatenate([
                jnp.concatenate([right[pick[((d * 8 + i) * 2 + s) * 4 + t]] for t in range(OUT)], axis=1)
                for d in range(8) for s in range(SLOTS)], axis=0)
            total = jnp.dot(lhs, rhs, preferred_element_type=jnp.float32).astype(jnp.bfloat16)
            for t in range(OUT):
                stage[i, t] = total[:, t * BLOCK:(t + 1) * BLOCK]
    done = pltpu.make_async_copy(stage, out_hbm, out_sem)
    done.start()
    for copy in sent:
        copy.wait_send()
    done.wait()


def slot_of(d):
    return d


def slot_of_row(d):
    dz, dc = d // 2, d % 2
    return ((4 - dz) % 4) * 2 + dc


def solution(mesh, parts=PARTS):
    def slot_of_q(d):
        return (d // 4) * 4 + (4 - d % 4) % 4

    globals()["slot_of"] = slot_of_q

    def step(*args):
        smem, hbm = pl.BlockSpec(memory_space=pltpu.SMEM), pl.BlockSpec(memory_space=pl.ANY)
        return pl.pallas_call(
            functools.partial(kernel, parts),
            out_shape=jax.ShapeDtypeStruct((ROWS, OUT, BLOCK, BLOCK), jnp.bfloat16),
            in_specs=[hbm, smem, smem, hbm, smem, smem, smem, smem, smem],
            out_specs=hbm,
            scratch_shapes=[
                pltpu.VMEM((8, ROWS, SLOTS, BLOCK, BLOCK), jnp.bfloat16),
                pltpu.VMEM((ROWS, SLOTS, BLOCK, BLOCK), jnp.bfloat16),
                pltpu.VMEM((65, BLOCK, BLOCK), jnp.bfloat16),
                pltpu.VMEM((ROWS, BLOCK, OUT * BLOCK), jnp.float32),
                pltpu.VMEM((ROWS, OUT, BLOCK, BLOCK), jnp.bfloat16),
                pltpu.SMEM((8, 128), jnp.int32),
                pltpu.SMEM((8, 128), jnp.int32),
                pltpu.SMEM((32,), jnp.int32),
                pltpu.SMEM((32,), jnp.int32),
                pltpu.SMEM((512,), jnp.int32),
                pltpu.SemaphoreType.DMA((N_COPIES,)),
                pltpu.SemaphoreType.DMA((N_COPIES,)),
                pltpu.SemaphoreType.DMA((2,)),
                pltpu.SemaphoreType.DMA,
            ],
            compiler_params=pltpu.CompilerParams(
                collective_id=0, has_side_effects=True, vmem_limit_bytes=48 * 1024 * 1024
            ),
        )(args[0], args[1], args[2], args[3].reshape(8, BLOCK, BLOCK), *args[4:])

    whole = P("row", "col", None, None)
    flat = P("row", "col")
    return jax.shard_map(
        step, mesh=mesh, in_specs=(whole, flat, flat, whole, flat, flat, flat, flat, P()),
        out_specs=whole, check_vma=False,
    )
```

time: 412 us -> 78.8 us (0.19)
  the two profiles are of different devices: /device:TPU:65 before, /device:TPU:64 now
where the time goes in v1:
time: 78.8 us; the launch traced here: 78.4 us
  Pallas kernels  72 us (91%)
  local copies, waits for them, and re-layouts  6.45 us (8%)
    pallas_call x1, Pallas kernels, step(): pl.pallas_call(functools.partial(kernel, parts), out_shape=jax.ShapeDtype...  72 us
    unnamed x25, local copies, waits for them, and re-layouts  6.45 us

profile of v1, /device:TPU:64, one launch (start us, length us, event | category | flops | bytes accessed | tf_op | source)
XLA Modules:
  0.0 78.4 jit_solution(16890886422789231575)
XLA Ops:
  0.0 0.0 copy-start.4
  0.0 0.7 copy-done.4
  0.7 0.0 copy-start.6
  0.7 0.1 copy.12.rcol
  0.8 0.6 copy-done.6
  1.3 0.0 copy-start.5
  1.3 0.1 copy.13.rcount
  1.4 0.6 copy-done.5
  2.0 0.0 copy-start.7
  2.0 0.0 copy-start.3
  2.0 0.1 copy.10.lcol
  2.1 0.6 copy-done.7
  2.7 0.0 copy-start.2
  2.7 0.1 copy.11.lcount
  2.8 0.0 copy-done.3
  2.8 0.0 copy-start.8
  2.8 0.1 copy.14.ocol
  2.8 0.6 copy-done.8
  3.4 0.1 copy.15.ocount
  3.5 0.0 copy-done.2
  3.5 0.0 copy-start
  3.5 1.0 %copy-done = bf16[8,2,128,128]{3,2,1,0:T(8,128)(2,1)S(1)} copy-done((bf16[8,2,128,128]{3,2,1,0:T(8,128)(2,1)S(1)}, bf16[8,2,128,128]{3,2,1,0:T(8,128)(2,1)}, u32[]{:S(2)}) %copy-start) | copy-done | bytes 524312
  4.5 0.0 copy-start.1
  4.5 0.9 %copy-done.1 = bf16[4,2,128,128]{3,2,1,0:T(8,128)(2,1)S(1)} copy-done((bf16[4,2,128,128]{3,2,1,0:T(8,128)(2,1)S(1)}, bf16[4,2,128,128]{3,2,1,0:T(8,128)(2,1)}, u32[]{:S(2)}) %copy-start.1) | copy-done | bytes 262168
  5.5 72.0 %shard_map.91 = bf16[8,4,128,128]{3,2,1,0:T(8,128)(2,1)S(1)} custom-call(bf16[8,2,128,128]{3,2,1,0:T(8,128)(2,1)S(1)} %copy-done, s32[8,2]{1,0:T(8,128)S(1)} %copy.10.lcol, s32[8,1]{1,0:T(8,128)S(1)} %copy.11.lcount, bf16[8,128,128]{2,1,0:T(8,128)(2,1)S(1)} %bitcast.1, s32[4,2]{1,0:T(4,128)S(1)} %copy.12.rcol, s32[4,1]{1,0:T(4,128)S(1)} %copy.13.rcount, ...), custom_call_target="tpu_custom_call" | custom-call | tf_op jit(solution)/shard_map/pallas_call | solution.py:270
  77.5 1.0 %copy.17 = bf16[8,4,128,128]{3,2,1,0:T(8,128)(2,1)} copy(bf16[8,4,128,128]{3,2,1,0:T(8,128)(2,1)S(1)} %shard_map.91) | data formatting | bytes 2097152
Async XLA Ops:
  0.0 0.7 copy-start.4
  0.7 0.7 copy-start.6
  1.3 0.7 copy-start.5
  2.0 0.7 copy-start.7
  2.0 0.7 copy-start.3
  2.7 0.8 %copy-start.2 = (s32[12,32]{1,0:T(8,128)S(1)}, s32[12,32]{1,0:T(8,128)}, u32[]{:S(2)}) copy-start(s32[12,32]{1,0:T(8,128)} %owner.1) | copy-start | bytes 4612
  2.8 0.7 copy-start.8
  3.5 1.0 %copy-start = (bf16[8,2,128,128]{3,2,1,0:T(8,128)(2,1)S(1)}, bf16[8,2,128,128]{3,2,1,0:T(8,128)(2,1)}, u32[]{:S(2)}) copy-start(bf16[8,2,128,128]{3,2,1,0:T(8,128)(2,1)} %left_hbm.1) | copy-start | bytes 1572868
  4.5 0.9 %copy-start.1 = (bf16[4,2,128,128]{3,2,1,0:T(8,128)(2,1)S(1)}, bf16[4,2,128,128]{3,2,1,0:T(8,128)(2,1)}, u32[]{:S(2)}) copy-start(bf16[4,2,128,128]{3,2,1,0:T(8,128)(2,1)} %param.12) | copy-start | bytes 786436

commit v2 on v0

v2 whole, which is shorter than its diff:
```python
import functools

import jax
import jax.numpy as jnp
from jax import lax
from jax.experimental import pallas as pl
from jax.experimental.pallas import tpu as pltpu
from jax.sharding import PartitionSpec as P

MESH = pl.DeviceIdType.MESH
ROWS, SLOTS, OUT, PANEL, BLOCK = 8, 2, 4, 4, 128
HALF = ROWS // 2
GROUP = 9
N_COPIES = 136
PARTS = ("x", "y", "z", "compute")


def kernel(
    parts,
    left_hbm, lcol_hbm, lcount_hbm, right_hbm, rcol_hbm, rcount_hbm, ocol_hbm, ocount_hbm, owner_hbm,
    out_hbm,
    left, relay, right, acc, stage,
    lcol, lcount, rcol, rcount, ocol, ocount, owner,
    lcode, rcode, ocode, place_vmem, place,
    send_sem, recv_sem, local_sem, small_sem, out_sem, ready,
):
    r = lax.axis_index("row")
    c = lax.axis_index("col")
    z, core = r // 2, r % 2
    x, y, low = c // 24, (c // 3) % 8, c % 3

    def at_q(dx, dy):
        return (r, ((x + dx) % 4) * 24 + ((y + dy) % 8) * 3 + low)

    def at_row(dz, dcore):
        return (((z + dz) % 4) * 2 + (core + dcore) % 2, c)

    east, west, north, south = at_q(1, 0), at_q(3, 0), at_q(0, 2), at_q(0, 6)
    up, down, twin = at_row(1, 0), at_row(3, 0), at_row(0, 1)

    barrier = pltpu.get_barrier_semaphore()

    def greet(device):
        pl.semaphore_signal(barrier, inc=1, device_id=device, device_id_type=MESH)

    for device in (east, west, north, south, twin):
        greet(device)
    pl.when(z != 3)(lambda: greet(up))
    pl.when(z == 0)(lambda: greet(down))
    own_left = pltpu.make_async_copy(left_hbm, left.at[0], local_sem.at[0])
    own_left.start()
    own_right = pltpu.make_async_copy(right_hbm, right.at[pl.ds(0, 8)], local_sem.at[1])
    own_right.start()
    small = [
        pltpu.make_async_copy(src, dst, small_sem.at[n])
        for n, (src, dst) in enumerate((
            (lcol_hbm, lcol), (lcount_hbm, lcount), (rcol_hbm, rcol), (rcount_hbm, rcount),
            (ocol_hbm, ocol), (ocount_hbm, ocount), (owner_hbm, owner)))
    ]
    for copy in small:
        copy.start()
    pl.semaphore_wait(barrier, 5 + jnp.where(z != 0, 1, 0) + jnp.where(z == 3, 1, 0))
    pl.when(z != 0)(lambda: pl.semaphore_signal(ready.at[0], inc=1, device_id=down, device_id_type=MESH))
    pl.when(z == 3)(lambda: pl.semaphore_signal(ready.at[1], inc=1, device_id=up, device_id_type=MESH))

    sent = []

    def remote(src, dst, device, start=True):
        n = len(sent)
        copy = pltpu.make_async_remote_copy(
            src_ref=src, dst_ref=dst, send_sem=send_sem.at[n], recv_sem=recv_sem.at[n],
            device_id=device, device_id_type=MESH,
        )
        if start:
            copy.start()
        sent.append(copy)
        return copy

    def row(ref, i):
        return ref.at[pl.ds(i, 1)]

    def rslot(dz, dc, k):
        return right.at[pl.ds((dz * 2 + dc) * GROUP + k * 2, 2)]

    events = []
    pending = {}

    def need(d, i, copy):
        pending.setdefault((d, i), []).append(copy)

    def at(when):
        return lambda run: events.append((when, len(events), run))

    order_e = list(range(ROWS))
    order_w = list(range(HALF, ROWS)) + list(range(HALF))
    alpha, beta = order_e[:HALF], order_e[HALF:]
    if "y" in parts:
        to_n = [remote(row(left_hbm, i), row(relay, i), north) for i in alpha]
        to_s = [remote(row(left_hbm, i), row(relay, i), south) for i in beta]
    if "x" in parts:
        to_e, to_w = {}, {}
        for a, b in zip(order_e, order_w):
            to_e[a] = remote(row(left_hbm, a), left.at[3, pl.ds(a, 1)], east)
            to_w[b] = remote(row(left_hbm, b), left.at[1, pl.ds(b, 1)], west)
    if "z" in parts:
        to_up = [remote(right_hbm.at[pl.ds(2 * k, 2)], rslot(3, 0, k), up, False) for k in (0, 1, 2, 3)]
        to_down = [remote(right_hbm.at[pl.ds(2 * k, 2)], rslot(1, 0, k), down, False) for k in (2, 3, 0, 1)]

        def start(copies):
            for copy in copies:
                copy.start()

        def start_late(copies, n):
            pl.semaphore_wait(ready.at[n], 1)
            start(copies)

        pl.when(z == 3)(lambda: start(to_up))
        pl.when(z != 0)(lambda: start(to_down))
        to_twin = remote(right_hbm, right.at[pl.ds(GROUP, 8)], twin)

    for copy in small:
        copy.wait()
    panel = (r + x * 2 + y // 4) % 8
    for i in range(ROWS):
        for s in range(SLOTS):
            lcode[0, i * 2 + s] = jnp.where(s < lcount[0, i], panel * 4 + lcol[s, i], 32)
        for t in range(OUT):
            ocode[i * 4 + t] = jnp.where(t < ocount[0, i], ocol[t, i], 8)
    for k in range(PANEL):
        c0 = jnp.where(0 < rcount[0, k], rcol[0, k], -1)
        c1 = jnp.where(1 < rcount[0, k], rcol[1, k], -1)
        for n in range(8):
            rcode[0, k * 16 + n] = jnp.where(c0 == n, k * 2, jnp.where(c1 == n, k * 2 + 1, 8))
        rcode[0, k * 16 + 8] = 8
    for n in range(9):
        rcode[0, PANEL * 16 + n] = 8
    if "x" in parts:
        code_e = remote(lcode.at[0], lcode.at[3], east)
        code_w = remote(lcode.at[0], lcode.at[1], west)
    if "y" in parts:
        code_n = remote(lcode.at[0], lcode.at[8], north)
    if "z" in parts:
        code_up = remote(rcode.at[0], rcode.at[6], up, False)
        code_down = remote(rcode.at[0], rcode.at[2], down, False)
        to_up.append(code_up)
        to_down.append(code_down)
        pl.when(z == 3)(code_up.start)
        pl.when(z != 0)(code_down.start)
        code_twin = remote(rcode.at[0], rcode.at[1], twin)
    region = (y % 4) * 3 + low
    lane = lax.broadcasted_iota(jnp.int32, (1, 128), 1)
    owners = jnp.full((1, 128), 0, jnp.int32)
    for e in range(32):
        owners = jnp.where(lane == e, owner[region, e], owners)
    rank = jnp.zeros((1, 128), jnp.int32)
    for e in range(32):
        rank += jnp.where((owners == owner[region, e]) & (lane > e), 1, 0)
    rank = jnp.minimum(rank, 3)
    slot = (((owners >> 1) - z) & 3) * 2 + ((owners + core) & 1)
    place_vmem[pl.ds(0, 1), :] = jnp.where(lane < 32, slot, 0)
    place_vmem[pl.ds(1, 1), :] = jnp.where(lane < 32, rank, 4) * 16
    placed = pltpu.make_async_copy(place_vmem, place, local_sem.at[2])
    placed.start()
    for n in range(8):
        right[pl.ds(n * GROUP + 8, 1)] = jnp.zeros((1, BLOCK, BLOCK), jnp.bfloat16)

    def ring(d, i, e, w, when):
        @at(when)
        def _():
            if i in alpha:
                e.wait_recv()
                need(d + 2, i, remote(left.at[d + 3, pl.ds(i, 1)], left.at[d + 2, pl.ds(i, 1)], east))
                need(d + 1, i, w)
            else:
                w.wait_recv()
                need(d + 2, i, remote(left.at[d + 1, pl.ds(i, 1)], left.at[d + 2, pl.ds(i, 1)], west))
                need(d + 3, i, e)

    codes = []
    if "x" in parts:
        for j in range(HALF):
            ring(0, alpha[j], to_e[alpha[j]], to_w[alpha[j]], 3 + 1.5 * j)
            ring(0, beta[j], to_e[beta[j]], to_w[beta[j]], 3 + 1.5 * j)

        @at(7.6)
        def _():
            code_e.wait_recv()
            codes.extend([remote(lcode.at[3], lcode.at[2], east), code_w])
    if "y" in parts:
        crossed = {}

        def crossing(j):
            @at(5 + 2.7 * j)
            def _():
                to_n[j].wait_recv()
                crossed[alpha[j]] = remote(row(relay, alpha[j]), left.at[4, pl.ds(alpha[j], 1)], north)
                to_s[j].wait_recv()
                crossed[beta[j]] = remote(row(relay, beta[j]), left.at[4, pl.ds(beta[j], 1)], south)
                if j == HALF - 1:
                    code_n.wait_recv()
                    crossed["code"] = remote(lcode.at[8], lcode.at[4], north)

            @at(14.5 + 2.7 * j)
            def _():
                for i in (alpha[j], beta[j]):
                    crossed[i].wait_recv()
                    if "x" not in parts:
                        continue
                    e = remote(left.at[4, pl.ds(i, 1)], left.at[7, pl.ds(i, 1)], east)
                    w = remote(left.at[4, pl.ds(i, 1)], left.at[5, pl.ds(i, 1)], west)
                    passed[i] = (e, w)
                if j == HALF - 1:
                    crossed["code"].wait_recv()
                    if "x" in parts:
                        passed["code"] = (
                            remote(lcode.at[4], lcode.at[7], east), remote(lcode.at[4], lcode.at[5], west))

            @at(20 + 3.5 * j)
            def _():
                if "x" not in parts:
                    return
                for i in (alpha[j], beta[j]):
                    e, w = passed[i]
                    if i in alpha:
                        e.wait_recv()
                        need(6, i, remote(left.at[7, pl.ds(i, 1)], left.at[6, pl.ds(i, 1)], east))
                        need(5, i, w)
                    else:
                        w.wait_recv()
                        need(6, i, remote(left.at[5, pl.ds(i, 1)], left.at[6, pl.ds(i, 1)], west))
                        need(7, i, e)
                if j == HALF - 1:
                    e, w = passed["code"]
                    e.wait_recv()
                    codes.extend([remote(lcode.at[7], lcode.at[6], east), w])

        passed = {}
        for j in range(HALF):
            crossing(j)

    if "z" in parts:
        at(4)(lambda: pl.when(z != 3)(lambda: start_late(to_up, 0)))
        at(9)(lambda: pl.when(z == 0)(lambda: start_late(to_down, 1)))
        over_up = [remote(rslot(3, 0, k), rslot(2, 0, k), up, False) for k in (0, 1)]
        over_down = [remote(rslot(1, 0, k), rslot(2, 0, k), down, False) for k in (2, 3)]
        over_code = remote(rcode.at[6], rcode.at[4], up, False)
        share_3 = [remote(rslot(3, 0, k), rslot(3, 1, k), twin, False) for k in (0, 1, 2, 3)]
        share_1 = [remote(rslot(1, 0, k), rslot(1, 1, k), twin, False) for k in (2, 3, 0, 1)]
        share_2 = [remote(rslot(2, 0, k), rslot(2, 1, k), twin, False) for k in (0, 1, 2, 3)]
        share_code = [remote(rcode.at[2 * d], rcode.at[2 * d + 1], twin, False) for d in (1, 2, 3)]

        def from_below(n):
            to_up[n].wait_recv()
            if n < 2:
                over_up[n].start()
            share_3[n].start()
            if n == 3:
                code_up.wait_recv()
                over_code.start()
                share_code[2].start()

        def from_above(n):
            to_down[n].wait_recv()
            if n < 2:
                over_down[n].start()
            share_1[n].start()
            if n == 3:
                code_down.wait_recv()
                share_code[0].start()

        for n in range(4):
            at(8.5 + 2.5 * n)(functools.partial(lambda n: pl.when(z != 0)(lambda: from_below(n)), n))
            at(19 + 2 * n)(functools.partial(lambda n: pl.when(z == 0)(lambda: from_below(n)), n))
            at(11 + 2.5 * n)(functools.partial(from_above, n))

        @at(27)
        def _():
            for n, copy in enumerate(over_up + over_down):
                copy.wait_recv()
                share_2[n].start()
            over_code.wait_recv()
            share_code[1].start()

        def right_done():
            own_right.wait()
            to_twin.wait_recv()
            code_twin.wait_recv()
            for copy in share_3 + share_1 + share_2 + share_code:
                copy.wait_recv()
            placed.wait()
    else:
        def right_done():
            own_right.wait()
            placed.wait()

    def product(i, ds):
        lhs = jnp.concatenate([left[d, i, s] for d in ds for s in range(SLOTS)], axis=1)
        rhs = []
        for d in ds:
            for s in range(SLOTS):
                k = lcode[d, i * 2 + s]
                where, first = place[0, k], place[1, k]
                rhs.append(jnp.concatenate([
                    right[where * GROUP + rcode[where, first + ocode[i * 4 + t]]] for t in range(OUT)], axis=1))
        return jnp.dot(lhs, jnp.concatenate(rhs, axis=0), preferred_element_type=jnp.float32)

    def settle(ds, rows):
        for d in ds:
            for i in rows:
                for copy in pending.pop((d, i), []):
                    copy.wait_recv()

    for _, _, run in sorted(events, key=lambda e: e[:2]):
        run()
    own_left.wait()
    right_done()
    for copy in codes:
        copy.wait_recv()
    settle(range(8), range(ROWS))
    if "compute" in parts:
        @pl.loop(0, ROWS)
        def _(i):
            total = product(i, range(8)).astype(jnp.bfloat16)
            for t in range(OUT):
                stage[i, t] = total[:, t * BLOCK:(t + 1) * BLOCK]
            pltpu.make_async_copy(stage.at[i], out_hbm.at[i], out_sem.at[i]).start()
        for i in range(ROWS):
            pltpu.make_async_copy(stage.at[i], out_hbm.at[i], out_sem.at[i]).wait()
    for copy in sent:
        copy.wait_send()


def solution(mesh, parts=PARTS):
    def step(*args):
        hbm = pl.BlockSpec(memory_space=pl.ANY)
        return pl.pallas_call(
            functools.partial(kernel, parts),
            out_shape=jax.ShapeDtypeStruct((ROWS, OUT, BLOCK, BLOCK), jnp.bfloat16),
            in_specs=[hbm] * 9,
            out_specs=hbm,
            scratch_shapes=[
                pltpu.VMEM((8, ROWS, SLOTS, BLOCK, BLOCK), jnp.bfloat16),
                pltpu.VMEM((ROWS, SLOTS, BLOCK, BLOCK), jnp.bfloat16),
                pltpu.VMEM((8 * GROUP, BLOCK, BLOCK), jnp.bfloat16),
                pltpu.VMEM((ROWS, BLOCK, OUT * BLOCK), jnp.float32),
                pltpu.VMEM((ROWS, OUT, BLOCK, BLOCK), jnp.bfloat16),
                pltpu.SMEM((SLOTS, ROWS), jnp.int32),
                pltpu.SMEM((1, ROWS), jnp.int32),
                pltpu.SMEM((2, PANEL), jnp.int32),
                pltpu.SMEM((1, PANEL), jnp.int32),
                pltpu.SMEM((OUT, ROWS), jnp.int32),
                pltpu.SMEM((1, ROWS), jnp.int32),
                pltpu.SMEM((12, 32), jnp.int32),
                pltpu.SMEM((9, 128), jnp.int32),
                pltpu.SMEM((8, 128), jnp.int32),
                pltpu.SMEM((32,), jnp.int32),
                pltpu.VMEM((2, 128), jnp.int32),
                pltpu.SMEM((2, 128), jnp.int32),
                pltpu.SemaphoreType.DMA((N_COPIES,)),
                pltpu.SemaphoreType.DMA((N_COPIES,)),
                pltpu.SemaphoreType.DMA((3,)),
                pltpu.SemaphoreType.DMA((7,)),
                pltpu.SemaphoreType.DMA((ROWS,)),
                pltpu.SemaphoreType.REGULAR((2,)),
            ],
            compiler_params=pltpu.CompilerParams(
                collective_id=0, has_side_effects=True, vmem_limit_bytes=58 * 1024 * 1024
            ),
        )(args[0], args[1].T, args[2].T, args[3].reshape(8, BLOCK, BLOCK), args[4].T, args[5].T, args[6].T,
          args[7].T, args[8])

    whole = P("row", "col", None, None)
    flat = P("row", "col")
    return jax.shard_map(
        step, mesh=mesh, in_specs=(whole, flat, flat, whole, flat, flat, flat, flat, P()),
        out_specs=whole, check_vma=False,
    )
```

time: 412 us -> 62.6 us (0.15)
  the two profiles are of different devices: /device:TPU:65 before, /device:TPU:16 now
where the time goes in v2:
time: 62.6 us; the launch traced here: 62.4 us
  Pallas kernels  60.1 us (96%)
  local copies, waits for them, and re-layouts  2.31 us (4%)
    pallas_call x1, Pallas kernels, step(): pl.pallas_call(functools.partial(kernel, parts), out_shape=jax.ShapeDtype...  60.1 us
    unnamed x1, local copies, waits for them, and re-layouts  2.31 us

profile of v2, /device:TPU:16, one launch (start us, length us, event | category | flops | bytes accessed | tf_op | source)
XLA Modules:
  0.0 62.4 jit_solution(9427319127643081828)
XLA Ops:
  0.0 60.1 %shard_map.91 = bf16[8,4,128,128]{3,2,1,0:T(8,128)(2,1)} custom-call(bf16[8,2,128,128]{3,2,1,0:T(8,128)(2,1)} %left_hbm.1, s32[2,8]{1,0:T(2,128)} %bitcast.9, s32[1,8]{1,0:T(1,128)} %bitcast.11, bf16[8,128,128]{2,1,0:T(8,128)(2,1)} %bitcast.7, s32[2,4]{1,0:T(2,128)} %bitcast.10, s32[1,4]{1,0:T(1,128)} %bitcast.12, s32[4,8]{1,0:T(4,128)} %bitcast.8, ...), custom_call_target="tpu_custom_call" | custom-call | tf_op jit(solution)/shard_map/pallas_call | solution.py:336
  60.1 2.3 %copy.11 = bf16[8,4,128,128]{3,2,1,0:T(8,128)(2,1)} copy(bf16[8,4,128,128]{3,2,1,0:T(8,128)(2,1)} %shard_map.91) | data formatting | bytes 2097152

commit v3 on v2

v3 whole, which is shorter than its diff:
```python
import functools

import jax
import jax.numpy as jnp
from jax import lax
from jax.experimental import pallas as pl
from jax.experimental.pallas import tpu as pltpu
from jax.sharding import PartitionSpec as P

MESH = pl.DeviceIdType.MESH
ROWS, SLOTS, OUT, PANEL, BLOCK = 8, 2, 4, 4, 128
HALF = ROWS // 2
GROUP = 9
N_COPIES = 136
PARTS = ("x", "y", "z", "compute")


def kernel(
    parts,
    left_hbm, lcol_hbm, lcount_hbm, right_hbm, rcol_hbm, rcount_hbm, ocol_hbm, ocount_hbm, owner_hbm,
    out_hbm,
    left, relay, right, acc, stage,
    lcol, lcount, rcol, rcount, ocol, ocount, owner,
    lcode, rcode, ocode, place_vmem, place, pick,
    send_sem, recv_sem, local_sem, small_sem, out_sem, ready,
):
    r = lax.axis_index("row")
    c = lax.axis_index("col")
    z, core = r // 2, r % 2
    x, y, low = c // 24, (c // 3) % 8, c % 3

    def at_q(dx, dy):
        return (r, ((x + dx) % 4) * 24 + ((y + dy) % 8) * 3 + low)

    def at_row(dz, dcore):
        return (((z + dz) % 4) * 2 + (core + dcore) % 2, c)

    east, west, north, south = at_q(1, 0), at_q(3, 0), at_q(0, 2), at_q(0, 6)
    up, down, twin = at_row(1, 0), at_row(3, 0), at_row(0, 1)

    def is_first(dx, dy, dz, dc):
        return (
            ((x + dx) % 4 == 0) & ((y + dy) % 8 == 0) & (low == 0) & ((z + dz) % 4 == 0) & ((core + dc) % 2 == 0))

    first = is_first(0, 0, 0, 0)
    turn = y // 2
    neighbours = [east, west, north, south, twin, up, down]
    opposite = [1, 0, 3, 2, 4, 6, 5]
    later = [
        ((x != 3) | is_first(1, 0, 0, 0)) & ~first,
        ((x == 0) | is_first(3, 0, 0, 0)) & ~first,
        ((turn <= 1) | is_first(0, 2, 0, 0)) & ~first,
        ((turn == 0) | (turn == 3) | is_first(0, 6, 0, 0)) & ~first,
        ((core == 1) | is_first(0, 0, 0, 1)) & ~first,
        (z != 3) & ~first,
        (z == 0) | is_first(0, 0, 3, 0),
    ]
    barrier = pltpu.get_barrier_semaphore()

    def greet(device):
        pl.semaphore_signal(barrier, inc=1, device_id=device, device_id_type=MESH)

    def answer(n):
        pl.semaphore_signal(ready.at[opposite[n]], inc=1, device_id=neighbours[n], device_id_type=MESH)

    for n, device in enumerate(neighbours):
        pl.when(later[n])(functools.partial(greet, device))
    own_left = pltpu.make_async_copy(left_hbm, left.at[0], local_sem.at[0])
    own_left.start()
    own_right = pltpu.make_async_copy(right_hbm, right.at[pl.ds(0, 8)], local_sem.at[1])
    own_right.start()
    small = [
        pltpu.make_async_copy(src, dst, small_sem.at[n])
        for n, (src, dst) in enumerate((
            (lcol_hbm, lcol), (lcount_hbm, lcount), (rcol_hbm, rcol), (rcount_hbm, rcount),
            (ocol_hbm, ocol), (ocount_hbm, ocount), (owner_hbm, owner)))
    ]
    for copy in small:
        copy.start()
    earlier = sum(jnp.where(l, 0, 1) for l in later)
    pl.when(earlier > 0)(lambda: pl.semaphore_wait(barrier, earlier))
    for n in range(7):
        pl.when(~later[n])(functools.partial(answer, n))

    for copy in small:
        copy.wait()
    panel = (r + x * 2 + y // 4) % 8
    for i in range(ROWS):
        for s in range(SLOTS):
            lcode[0, i * 2 + s] = jnp.where(s < lcount[0, i], panel * 4 + lcol[s, i], 32)
        for t in range(OUT):
            ocode[i * 4 + t] = jnp.where(t < ocount[0, i], ocol[t, i], 8)
    for k in range(PANEL):
        c0 = jnp.where(0 < rcount[0, k], rcol[0, k], -1)
        c1 = jnp.where(1 < rcount[0, k], rcol[1, k], -1)
        for n in range(8):
            rcode[0, k * 16 + n] = jnp.where(c0 == n, k * 2, jnp.where(c1 == n, k * 2 + 1, 8))
        rcode[0, k * 16 + 8] = 8
    for n in range(9):
        rcode[0, PANEL * 16 + n] = 8
    sent = []

    def remote(src, dst, device, start=True):
        n = len(sent)
        copy = pltpu.make_async_remote_copy(
            src_ref=src, dst_ref=dst, send_sem=send_sem.at[n], recv_sem=recv_sem.at[n],
            device_id=device, device_id_type=MESH,
        )
        if start:
            copy.start()
        sent.append(copy)
        return copy

    def row(ref, i):
        return ref.at[pl.ds(i, 1)]

    def rslot(dz, dc, k):
        return right.at[pl.ds((dz * 2 + dc) * GROUP + k * 2, 2)]

    events = []
    pending = {}

    def need(d, i, copy):
        pending.setdefault((d, i), []).append(copy)

    def at(when):
        return lambda run: events.append((when, len(events), run))

    order_e = list(range(ROWS))
    order_w = list(range(HALF, ROWS)) + list(range(HALF))
    alpha, beta = order_e[:HALF], order_e[HALF:]
    code_up = remote(rcode.at[0], rcode.at[6], up, False)
    code_down = remote(rcode.at[0], rcode.at[2], down, False)
    code_twin = remote(rcode.at[0], rcode.at[1], twin, False)
    code_e = remote(lcode.at[0], lcode.at[3], east, False)
    code_w = remote(lcode.at[0], lcode.at[1], west, False)
    code_n = remote(lcode.at[0], lcode.at[8], north, False)
    to_up = [remote(right_hbm.at[pl.ds(2 * k, 2)], rslot(3, 0, k), up, False) for k in (0, 1, 2, 3)]
    to_down = [remote(right_hbm.at[pl.ds(2 * k, 2)], rslot(1, 0, k), down, False) for k in (2, 3, 0, 1)]
    to_e = {i: remote(row(left_hbm, i), left.at[3, pl.ds(i, 1)], east, False) for i in order_e}
    to_w = {i: remote(row(left_hbm, i), left.at[1, pl.ds(i, 1)], west, False) for i in order_w}
    to_n = [remote(row(left_hbm, i), row(relay, i), north, False) for i in alpha]
    to_s = [remote(row(left_hbm, i), row(relay, i), south, False) for i in beta]
    to_twin = remote(right_hbm, right.at[pl.ds(GROUP, 8)], twin, False)
    groups = [
        [code_e] + list(to_e.values()), [code_w] + list(to_w.values()), [code_n] + to_n, to_s,
        [code_twin, to_twin], [code_up] + to_up, [code_down] + to_down]

    def start(copies):
        for copy in copies:
            copy.start()

    def start_late(n):
        pl.semaphore_wait(ready.at[n], 1)
        start(groups[n])

    for n in (5, 6, 0, 1, 2, 3, 4):
        pl.when(~later[n])(functools.partial(start, groups[n]))
    for n in (0, 1, 2, 3, 4):
        pl.when(later[n])(functools.partial(start_late, n))

    region = (y % 4) * 3 + low
    lane = lax.broadcasted_iota(jnp.int32, (1, 128), 1)
    owners = jnp.full((1, 128), 0, jnp.int32)
    for e in range(32):
        owners = jnp.where(lane == e, owner[region, e], owners)
    rank = jnp.zeros((1, 128), jnp.int32)
    for e in range(32):
        rank += jnp.where((owners == owner[region, e]) & (lane > e), 1, 0)
    rank = jnp.minimum(rank, 3)
    slot = (((owners >> 1) - z) & 3) * 2 + ((owners + core) & 1)
    place_vmem[pl.ds(0, 1), :] = jnp.where(lane < 32, slot, 0)
    place_vmem[pl.ds(1, 1), :] = jnp.where(lane < 32, rank, 4) * 16
    placed = pltpu.make_async_copy(place_vmem, place, local_sem.at[2])
    placed.start()
    for n in range(8):
        right[pl.ds(n * GROUP + 8, 1)] = jnp.zeros((1, BLOCK, BLOCK), jnp.bfloat16)

    def ring(d, i, e, w, when):
        @at(when)
        def _():
            if i in alpha:
                e.wait_recv()
                need(d + 2, i, remote(left.at[d + 3, pl.ds(i, 1)], left.at[d + 2, pl.ds(i, 1)], east))
                need(d + 1, i, w)
            else:
                w.wait_recv()
                need(d + 2, i, remote(left.at[d + 1, pl.ds(i, 1)], left.at[d + 2, pl.ds(i, 1)], west))
                need(d + 3, i, e)

    codes = []
    if "x" in parts:
        for j in range(HALF):
            ring(0, alpha[j], to_e[alpha[j]], to_w[alpha[j]], 3 + 1.5 * j)
            ring(0, beta[j], to_e[beta[j]], to_w[beta[j]], 3 + 1.5 * j)

        @at(7.6)
        def _():
            code_e.wait_recv()
            codes.extend([remote(lcode.at[3], lcode.at[2], east), code_w])
    if "y" in parts:
        crossed = {}

        def crossing(j):
            @at(5 + 2.7 * j)
            def _():
                to_n[j].wait_recv()
                crossed[alpha[j]] = remote(row(relay, alpha[j]), left.at[4, pl.ds(alpha[j], 1)], north)
                to_s[j].wait_recv()
                crossed[beta[j]] = remote(row(relay, beta[j]), left.at[4, pl.ds(beta[j], 1)], south)
                if j == 0:
                    code_n.wait_recv()
                    crossed["code"] = remote(lcode.at[8], lcode.at[4], north)

            @at(14.5 + 2.7 * j)
            def _():
                for i in (alpha[j], beta[j]):
                    crossed[i].wait_recv()
                    if "x" not in parts:
                        continue
                    e = remote(left.at[4, pl.ds(i, 1)], left.at[7, pl.ds(i, 1)], east)
                    w = remote(left.at[4, pl.ds(i, 1)], left.at[5, pl.ds(i, 1)], west)
                    passed[i] = (e, w)
                if j == 0:
                    crossed["code"].wait_recv()
                    if "x" in parts:
                        passed["code"] = (
                            remote(lcode.at[4], lcode.at[7], east), remote(lcode.at[4], lcode.at[5], west))

            @at(20 + 3.5 * j)
            def _():
                if "x" not in parts:
                    return
                for i in (alpha[j], beta[j]):
                    e, w = passed[i]
                    if i in alpha:
                        e.wait_recv()
                        need(6, i, remote(left.at[7, pl.ds(i, 1)], left.at[6, pl.ds(i, 1)], east))
                        need(5, i, w)
                    else:
                        w.wait_recv()
                        need(6, i, remote(left.at[5, pl.ds(i, 1)], left.at[6, pl.ds(i, 1)], west))
                        need(7, i, e)
                if j == 0:
                    e, w = passed["code"]
                    e.wait_recv()
                    codes.extend([remote(lcode.at[7], lcode.at[6], east), w])

        passed = {}
        for j in range(HALF):
            crossing(j)

    if "z" in parts:
        at(4)(lambda: pl.when(later[5])(lambda: start_late(5)))
        at(9)(lambda: pl.when(later[6])(lambda: start_late(6)))
        over_up = [remote(rslot(3, 0, k), rslot(2, 0, k), up, False) for k in (0, 1)]
        over_down = [remote(rslot(1, 0, k), rslot(2, 0, k), down, False) for k in (2, 3)]
        over_code = remote(rcode.at[6], rcode.at[4], up, False)
        share_3 = [remote(rslot(3, 0, k), rslot(3, 1, k), twin, False) for k in (0, 1, 2, 3)]
        share_1 = [remote(rslot(1, 0, k), rslot(1, 1, k), twin, False) for k in (2, 3, 0, 1)]
        share_2 = [remote(rslot(2, 0, k), rslot(2, 1, k), twin, False) for k in (0, 1, 2, 3)]
        share_code = [remote(rcode.at[2 * d], rcode.at[2 * d + 1], twin, False) for d in (1, 2, 3)]

        def from_below(n):
            if n == 0:
                code_up.wait_recv()
                over_code.start()
                share_code[2].start()
            to_up[n].wait_recv()
            if n < 2:
                over_up[n].start()
            share_3[n].start()

        def from_above(n):
            if n == 0:
                code_down.wait_recv()
                share_code[0].start()
            to_down[n].wait_recv()
            if n < 2:
                over_down[n].start()
            share_1[n].start()

        def code_over():
            over_code.wait_recv()
            share_code[1].start()

        def from_across():
            for n, copy in enumerate(over_up + over_down):
                copy.wait_recv()
                share_2[n].start()

        for n in range(4):
            at((10, 16, 24, 27.2)[n])(functools.partial(lambda n: pl.when(z != 0)(lambda: from_below(n)), n))
            at((20, 25, 31.5, 31.6)[n])(functools.partial(lambda n: pl.when(z == 0)(lambda: from_below(n)), n))
            at((10.5, 16.5, 24, 27.2)[n])(functools.partial(from_above, n))
        at(20.5)(code_over)
        at(31.8)(from_across)

        def codes_done():
            code_twin.wait_recv()
            for copy in share_code + codes:
                copy.wait_recv()
            placed.wait()

        def right_done():
            own_right.wait()
            to_twin.wait_recv()
            for copy in share_3 + share_1 + share_2:
                copy.wait_recv()
    else:
        def right_done():
            pl.when(z != 3)(lambda: pl.semaphore_wait(ready.at[0], 1))
            pl.when(z == 0)(lambda: pl.semaphore_wait(ready.at[1], 1))
            own_right.wait()

        def codes_done():
            for copy in codes:
                copy.wait_recv()
            placed.wait()

    def picks(first):
        if first == 0:
            codes_done()

        @pl.loop(first, first + HALF)
        def _(i):
            for d in range(8):
                for s in range(SLOTS):
                    k = lcode[d, i * 2 + s]
                    where, at = place[0, k], place[1, k]
                    for t in range(OUT):
                        pick[i * 64 + (d * 2 + s) * 4 + t] = where * GROUP + rcode[where, at + ocode[i * 4 + t]]

    events.append((23.7, 900, lambda: picks(0)))
    events.append((27.1, 901, lambda: picks(HALF)))

    def product(i, ds, half):
        total = jnp.zeros((BLOCK, 2 * BLOCK), jnp.float32)
        for d in ds:
            lhs = jnp.concatenate([left[d, i, s] for s in range(SLOTS)], axis=1)
            rhs = jnp.concatenate([
                jnp.concatenate([right[pick[i * 64 + (d * 2 + s) * 4 + half * 2 + t]] for t in range(2)], axis=1)
                for s in range(SLOTS)], axis=0)
            total += jnp.dot(lhs, rhs, preferred_element_type=jnp.float32)
        return total

    def settle(ds, rows):
        for d in ds:
            for i in rows:
                for copy in pending.pop((d, i), []):
                    copy.wait_recv()

    for _, _, run in sorted(events, key=lambda e: e[:2]):
        run()
    own_left.wait()
    right_done()
    settle(range(4), range(ROWS))
    if "compute" in parts:
        @pl.loop(0, ROWS)
        def _(i):
            for half in range(2):
                acc[i, half] = product(i, range(4), half)
    for j in range(HALF):
        settle(range(4, 8), (j, j + HALF))
        if "compute" in parts:
            @pl.loop(0, 2)
            def _(h):
                i = j + h * HALF
                for half in range(2):
                    total = (acc[i, half] + product(i, range(4, 8), half)).astype(jnp.bfloat16)
                    for t in range(2):
                        stage[i, half * 2 + t] = total[:, t * BLOCK:(t + 1) * BLOCK]
                pltpu.make_async_copy(stage.at[i], out_hbm.at[i], out_sem.at[i]).start()
    if "compute" in parts:
        for i in range(ROWS):
            pltpu.make_async_copy(stage.at[i], out_hbm.at[i], out_sem.at[i]).wait()
    for copy in sent:
        copy.wait_send()


def solution(mesh, parts=PARTS):
    def step(*args):
        hbm = pl.BlockSpec(memory_space=pl.ANY)
        return pl.pallas_call(
            functools.partial(kernel, parts),
            out_shape=jax.ShapeDtypeStruct((ROWS, OUT, BLOCK, BLOCK), jnp.bfloat16),
            in_specs=[hbm] * 9,
            out_specs=hbm,
            scratch_shapes=[
                pltpu.VMEM((8, ROWS, SLOTS, BLOCK, BLOCK), jnp.bfloat16),
                pltpu.VMEM((ROWS, SLOTS, BLOCK, BLOCK), jnp.bfloat16),
                pltpu.VMEM((8 * GROUP, BLOCK, BLOCK), jnp.bfloat16),
                pltpu.VMEM((ROWS, 2, BLOCK, 2 * BLOCK), jnp.float32),
                pltpu.VMEM((ROWS, OUT, BLOCK, BLOCK), jnp.bfloat16),
                pltpu.SMEM((SLOTS, ROWS), jnp.int32),
                pltpu.SMEM((1, ROWS), jnp.int32),
                pltpu.SMEM((2, PANEL), jnp.int32),
                pltpu.SMEM((1, PANEL), jnp.int32),
                pltpu.SMEM((OUT, ROWS), jnp.int32),
                pltpu.SMEM((1, ROWS), jnp.int32),
                pltpu.SMEM((12, 32), jnp.int32),
                pltpu.SMEM((9, 128), jnp.int32),
                pltpu.SMEM((8, 128), jnp.int32),
                pltpu.SMEM((32,), jnp.int32),
                pltpu.VMEM((2, 128), jnp.int32),
                pltpu.SMEM((2, 128), jnp.int32),
                pltpu.SMEM((512,), jnp.int32),
                pltpu.SemaphoreType.DMA((N_COPIES,)),
                pltpu.SemaphoreType.DMA((N_COPIES,)),
                pltpu.SemaphoreType.DMA((3,)),
                pltpu.SemaphoreType.DMA((7,)),
                pltpu.SemaphoreType.DMA((ROWS,)),
                pltpu.SemaphoreType.REGULAR((7,)),
            ],
            compiler_params=pltpu.CompilerParams(
                collective_id=0, has_side_effects=True, vmem_limit_bytes=58 * 1024 * 1024
            ),
        )(args[0], args[1].T, args[2].T, args[3].reshape(8, BLOCK, BLOCK), args[4].T, args[5].T, args[6].T,
          args[7].T, args[8])

    whole = P("row", "col", None, None)
    flat = P("row", "col")
    return jax.shard_map(
        step, mesh=mesh, in_specs=(whole, flat, flat, whole, flat, flat, flat, flat, P()),
        out_specs=whole, check_vma=False,
    )
```

time: 62.6 us -> 57 us (0.911)
  the two profiles are of different devices: /device:TPU:16 before, /device:TPU:49 now
where the time goes in v3:
time: 57 us; the launch traced here: 56.8 us
  Pallas kernels  54.5 us (96%)
  local copies, waits for them, and re-layouts  2.31 us (4%)
    pallas_call x1, Pallas kernels, step(): pl.pallas_call(functools.partial(kernel, parts), out_shape=jax.ShapeDtype...  54.5 us
    unnamed x1, local copies, waits for them, and re-layouts  2.31 us

profile of v3, /device:TPU:49, one launch (start us, length us, event | category | flops | bytes accessed | tf_op | source)
XLA Modules:
  0.0 56.8 jit_solution(15956559046901311100)
XLA Ops:
  0.0 54.5 %shard_map.91 = bf16[8,4,128,128]{3,2,1,0:T(8,128)(2,1)} custom-call(bf16[8,2,128,128]{3,2,1,0:T(8,128)(2,1)} %left_hbm.1, s32[2,8]{1,0:T(2,128)} %bitcast.9, s32[1,8]{1,0:T(1,128)} %bitcast.11, bf16[8,128,128]{2,1,0:T(8,128)(2,1)} %bitcast.7, s32[2,4]{1,0:T(2,128)} %bitcast.10, s32[1,4]{1,0:T(1,128)} %bitcast.12, s32[4,8]{1,0:T(4,128)} %bitcast.8, ...), custom_call_target="tpu_custom_call" | custom-call | tf_op jit(solution)/shard_map/pallas_call | solution.py:384
  54.5 2.3 %copy.11 = bf16[8,4,128,128]{3,2,1,0:T(8,128)(2,1)} copy(bf16[8,4,128,128]{3,2,1,0:T(8,128)(2,1)} %shard_map.91) | data formatting | bytes 2097152

commit v4 on v3

--- a/solution.py
+++ b/solution.py
@@ -82,6 +82,66 @@
     for n in range(7):
         pl.when(~later[n])(functools.partial(answer, n))
 
+    sent = []
+
+    def remote(src, dst, device, start=True):
+        n = len(sent)
+        copy = pltpu.make_async_remote_copy(
+            src_ref=src, dst_ref=dst, send_sem=send_sem.at[n], recv_sem=recv_sem.at[n],
+            device_id=device, device_id_type=MESH,
+        )
+        if start:
+            copy.start()
+        sent.append(copy)
+        return copy
+
+    def row(ref, i):
+        return ref.at[pl.ds(i, 1)]
+
+    def rslot(dz, dc, k):
+        return right.at[pl.ds((dz * 2 + dc) * GROUP + k * 2, 2)]
+
+    events = []
+    pending = {}
+
+    def need(d, i, copy):
+        pending.setdefault((d, i), []).append(copy)
+
+    def at(when):
+        return lambda run: events.append((when, len(events), run))
+
+    order_e = list(range(ROWS))
+    order_w = list(range(HALF, ROWS)) + list(range(HALF))
+    alpha, beta = order_e[:HALF], order_e[HALF:]
+    code_up = remote(rcode.at[0], rcode.at[6], up, False)
+    code_down = remote(rcode.at[0], rcode.at[2], down, False)
+    code_twin = remote(rcode.at[0], rcode.at[1], twin, False)
+    code_e = remote(lcode.at[0], lcode.at[3], east, False)
+    code_w = remote(lcode.at[0], lcode.at[1], west, False)
+    code_n = remote(lcode.at[0], lcode.at[8], north, False)
+    to_up = [remote(right_hbm.at[pl.ds(2 * k, 2)], rslot(3, 0, k), up, False) for k in (0, 1, 2, 3)]
+    to_down = [remote(right_hbm.at[pl.ds(2 * k, 2)], rslot(1, 0, k), down, False) for k in (2, 3, 0, 1)]
+    to_e = {i: remote(row(left_hbm, i), left.at[3, pl.ds(i, 1)], east, False) for i in order_e}
+    to_w = {i: remote(row(left_hbm, i), left.at[1, pl.ds(i, 1)], west, False) for i in order_w}
+    to_n = [remote(row(left_hbm, i), row(relay, i), north, False) for i in alpha]
+    to_s = [remote(row(left_hbm, i), row(relay, i), south, False) for i in beta]
+    to_twin = remote(right_hbm, right.at[pl.ds(GROUP, 8)], twin, False)
+    east_rows, west_rows = list(to_e.values()), list(to_w.values())
+    heads = [east_rows[:1], west_rows[:1], [], [], [], to_up[:0], to_down[:0]]
+    tails = [
+        [code_e] + east_rows[1:], [code_w] + west_rows[1:], [code_n] + to_n, to_s,
+        [code_twin, to_twin], [code_up] + to_up[0:], [code_down] + to_down[0:]]
+
+    def start(copies):
+        for copy in copies:
+            copy.start()
+
+    def start_late(n):
+        pl.semaphore_wait(ready.at[n], 1)
+        start(heads[n] + tails[n])
+
+    for n in (5, 6, 0, 1):
+        pl.when(~later[n])(functools.partial(start, heads[n]))
     for copy in small:
         copy.wait()
     panel = (r + x * 2 + y // 4) % 8
@@ -98,64 +158,8 @@
         rcode[0, k * 16 + 8] = 8
     for n in range(9):
         rcode[0, PANEL * 16 + n] = 8
-    sent = []
-
-    def remote(src, dst, device, start=True):
-        n = len(sent)
-        copy = pltpu.make_async_remote_copy(
-            src_ref=src, dst_ref=dst, send_sem=send_sem.at[n], recv_sem=recv_sem.at[n],
-            device_id=device, device_id_type=MESH,
-        )
-        if start:
-            copy.start()
-        sent.append(copy)
-        return copy
-
-    def row(ref, i):
-        return ref.at[pl.ds(i, 1)]
-
-    def rslot(dz, dc, k):
-        return right.at[pl.ds((dz * 2 + dc) * GROUP + k * 2, 2)]
-
-    events = []
-    pending = {}
-
-    def need(d, i, copy):
-        pending.setdefault((d, i), []).append(copy)
-
-    def at(when):
-        return lambda run: events.append((when, len(events), run))
-
-    order_e = list(range(ROWS))
-    order_w = list(range(HALF, ROWS)) + list(range(HALF))
-    alpha, beta = order_e[:HALF], order_e[HALF:]
-    code_up = remote(rcode.at[0], rcode.at[6], up, False)
-    code_down = remote(rcode.at[0], rcode.at[2], down, False)
-    code_twin = remote(rcode.at[0], rcode.at[1], twin, False)
-    code_e = remote(lcode.at[0], lcode.at[3], east, False)
-    code_w = remote(lcode.at[0], lcode.at[1], west, False)
-    code_n = remote(lcode.at[0], lcode.at[8], north, False)
-    to_up = [remote(right_hbm.at[pl.ds(2 * k, 2)], rslot(3, 0, k), up, False) for k in (0, 1, 2, 3)]
-    to_down = [remote(right_hbm.at[pl.ds(2 * k, 2)], rslot(1, 0, k), down, False) for k in (2, 3, 0, 1)]
-    to_e = {i: remote(row(left_hbm, i), left.at[3, pl.ds(i, 1)], east, False) for i in order_e}
-    to_w = {i: remote(row(left_hbm, i), left.at[1, pl.ds(i, 1)], west, False) for i in order_w}
-    to_n = [remote(row(left_hbm, i), row(relay, i), north, False) for i in alpha]
-    to_s = [remote(row(left_hbm, i), row(relay, i), south, False) for i in beta]
-    to_twin = remote(right_hbm, right.at[pl.ds(GROUP, 8)], twin, False)
-    groups = [
-        [code_e] + list(to_e.values()), [code_w] + list(to_w.values()), [code_n] + to_n, to_s,
-        [code_twin, to_twin], [code_up] + to_up, [code_down] + to_down]
-
-    def start(copies):
-        for copy in copies:
-            copy.start()
-
-    def start_late(n):
-        pl.semaphore_wait(ready.at[n], 1)
-        start(groups[n])
-
     for n in (5, 6, 0, 1, 2, 3, 4):
-        pl.when(~later[n])(functools.partial(start, groups[n]))
+        pl.when(~later[n])(functools.partial(start, tails[n]))
     for n in (0, 1, 2, 3, 4):
         pl.when(later[n])(functools.partial(start_late, n))
 

time: 57 us -> 55.6 us (0.975)
  the two profiles are of different devices: /device:TPU:49 before, /device:TPU:71 now
where the time goes in v4:
time: 55.6 us; the launch traced here: 55.4 us
  Pallas kernels  53.1 us (96%)
  local copies, waits for them, and re-layouts  2.31 us (4%)
    pallas_call x1, Pallas kernels, step(): pl.pallas_call(functools.partial(kernel, parts), out_shape=jax.ShapeDtype...  53.1 us
    unnamed x1, local copies, waits for them, and re-layouts  2.31 us

profile of v4, /device:TPU:71, one launch (start us, length us, event | category | flops | bytes accessed | tf_op | source)
XLA Modules:
  0.0 55.4 jit_solution(11525047811409687448)
XLA Ops:
  0.0 53.1 %shard_map.91 = bf16[8,4,128,128]{3,2,1,0:T(8,128)(2,1)} custom-call(bf16[8,2,128,128]{3,2,1,0:T(8,128)(2,1)} %left_hbm.1, s32[2,8]{1,0:T(2,128)} %bitcast.9, s32[1,8]{1,0:T(1,128)} %bitcast.11, bf16[8,128,128]{2,1,0:T(8,128)(2,1)} %bitcast.7, s32[2,4]{1,0:T(2,128)} %bitcast.10, s32[1,4]{1,0:T(1,128)} %bitcast.12, s32[4,8]{1,0:T(4,128)} %bitcast.8, ...), custom_call_target="tpu_custom_call" | custom-call | tf_op jit(solution)/shard_map/pallas_call | solution.py:388
  53.1 2.3 %copy.11 = bf16[8,4,128,128]{3,2,1,0:T(8,128)(2,1)} copy(bf16[8,4,128,128]{3,2,1,0:T(8,128)(2,1)} %shard_map.91) | data formatting | bytes 2097152

commit v5 on v4

--- a/solution.py
+++ b/solution.py
@@ -298,7 +298,9 @@
             at((20, 25, 31.5, 31.6)[n])(functools.partial(lambda n: pl.when(z == 0)(lambda: from_below(n)), n))
             at((10.5, 16.5, 24, 27.2)[n])(functools.partial(from_above, n))
         at(20.5)(code_over)
-        at(31.8)(from_across)
+        at(27.25)(lambda: pl.when(z >= 2)(from_across))
+        at(30.2)(lambda: pl.when(z == 1)(from_across))
+        at(31.8)(lambda: pl.when(z == 0)(from_across))
 
         def codes_done():
             code_twin.wait_recv()
@@ -347,6 +349,15 @@
                 for s in range(SLOTS)], axis=0)
             total += jnp.dot(lhs, rhs, preferred_element_type=jnp.float32)
         return total
+
+    gone = []
+
+    @at(30.3)
+    def _():
+        for copies in (heads[0], tails[0], heads[1], tails[1], tails[2], tails[3], tails[4]):
+            gone.extend(copies)
+        for copy in gone:
+            copy.wait_send()
 
     def settle(ds, rows):
         for d in ds:
@@ -375,11 +386,12 @@
                     for t in range(2):
                         stage[i, half * 2 + t] = total[:, t * BLOCK:(t + 1) * BLOCK]
                 pltpu.make_async_copy(stage.at[i], out_hbm.at[i], out_sem.at[i]).start()
+    for copy in sent:
+        if not any(copy is other for other in gone):
+            copy.wait_send()
     if "compute" in parts:
         for i in range(ROWS):
             pltpu.make_async_copy(stage.at[i], out_hbm.at[i], out_sem.at[i]).wait()
-    for copy in sent:
-        copy.wait_send()
 
 
 def solution(mesh, parts=PARTS):

time: 55.6 us -> 55.3 us (level)
  no operation moved by 1% of the time
where the time goes in v5:
time: 55.3 us; the launch traced here: 55.2 us
  Pallas kernels  52.8 us (95%)
  local copies, waits for them, and re-layouts  2.31 us (4%)
    pallas_call x1, Pallas kernels, step(): pl.pallas_call(functools.partial(kernel, parts), out_shape=jax.ShapeDtype...  52.8 us
    unnamed x1, local copies, waits for them, and re-layouts  2.31 us

profile of v5, /device:TPU:71, one launch (start us, length us, event | category | flops | bytes accessed | tf_op | source)
XLA Modules:
  0.0 55.2 jit_solution(4822630993242193893)
XLA Ops:
  0.0 52.8 %shard_map.91 = bf16[8,4,128,128]{3,2,1,0:T(8,128)(2,1)} custom-call(bf16[8,2,128,128]{3,2,1,0:T(8,128)(2,1)} %left_hbm.1, s32[2,8]{1,0:T(2,128)} %bitcast.9, s32[1,8]{1,0:T(1,128)} %bitcast.11, bf16[8,128,128]{2,1,0:T(8,128)(2,1)} %bitcast.7, s32[2,4]{1,0:T(2,128)} %bitcast.10, s32[1,4]{1,0:T(1,128)} %bitcast.12, s32[4,8]{1,0:T(4,128)} %bitcast.8, ...), custom_call_target="tpu_custom_call" | custom-call | tf_op jit(solution)/shard_map/pallas_call | solution.py:400
  52.8 2.3 %copy.11 = bf16[8,4,128,128]{3,2,1,0:T(8,128)(2,1)} copy(bf16[8,4,128,128]{3,2,1,0:T(8,128)(2,1)} %shard_map.91) | data formatting | bytes 2097152
